TPU v7x, 32 devices: a whole 2x2x4 slice. The times are simulated.
32 devices in a mesh: pair: 8 (over z, x), tp: 2 (over y), rep: 2 (over core).
Axes of the slice: x: 2, y: 2, z: 4, core: 2. Of those that a mesh axis runs over, the one named last changes fastest.
Arguments:
- normed: bfloat16 [2, 8, 8192], P(None, 'rep', 'pair'), parts along dimension 1, may hold values from -6 to 6
- w_query: bfloat16 [8192, 2048], P('pair', 'tp'), may hold values from -0.0625 to 0.0625
- b_query: float32 [2048], P('tp'), may hold values from -3 to 3
- w_key: bfloat16 [8192, 256], P('pair', 'tp'), may hold values from -0.25 to 0.25
- b_key: float32 [256], P('tp'), may hold values from -8 to 8
- w_value: bfloat16 [8192, 256], P('pair', 'tp'), may hold values from -0.0625 to 0.0625
- b_value: float32 [256], P('tp'), may hold values from -5 to 5
- w_out: bfloat16 [2048, 8192], P('tp', 'pair'), may hold values from -0.5 to 0.5
- pool: bfloat16 [16, 2, 512, 16, 256], P(('rep', 'pair'), 'tp'), parts along dimension 0, as said below
- page_table: int32 [16, 512], P(('rep', 'pair')), parts along dimension 0, may hold values from 0 to 511, as said below
- lengths: int32 [8], P('rep'), parts along dimension 0, may hold values from 8192 to 12286, as said below
- plan: int32 [8, 2], P('rep'), parts along dimension 0, may hold values from 0 to 64, as said below
Outputs:
- attended: float32 [2, 8, 8192], P(None, 'rep', 'pair'), parts along dimension 1
- new_pool: bfloat16 [16, 2, 512, 16, 256], P(('rep', 'pair'), 'tp'), parts along dimension 0
There are 2 independent parts, one for each index of `rep`. A program takes and returns all parts, laid end to end along the dimension named above; an argument that names none is the same for every part. Nothing has to cross between parts.
Inputs may be any that keep to these rules, and one draw needn't show every extreme that they name: `pool`: cached keys (first 128 entries of a slot row, already rotated) and values. `page_table`: each row is an order of the 512 slots of one pool. `lengths`: some request reaches the most. `plan`: some entry reaches the most.
All inputs are finite; a program needn't handle non-finite values.
Results may differ from a plain program's by a relative error of at most 0.011.
The roundings to bfloat16 on the way count: a program that leaves them out, or rounds other values in their place, can miss the bound.
Values may be sent and summed in bfloat16 or wider, within the bound.
No kernel may reach another device: no remote copies, remote signals or barrier semaphores. Data moves between devices by JAX's collectives and lax.ppermute only.
A program may use at most 64 MiB of HBM per device.

v0:
```python
import math

import jax
import jax.numpy as jnp
from jax import lax
from jax.experimental import pallas as pl
from jax.experimental.pallas import tpu as pltpu
from jax.sharding import PartitionSpec as P

PAGES_HALF = 384
STEPS = 2
SECTION = 64
MOVED_MAX = STEPS * SECTION
CHUNKS = 8
NEG = -1e30

rope_base = 1000000.0

VMEM = pl.BlockSpec(memory_space=pltpu.VMEM)
SMEM = pl.BlockSpec(memory_space=pltpu.SMEM)
HBM = pl.BlockSpec(memory_space=pltpu.HBM)


def params(mib):
    return pltpu.CompilerParams(vmem_limit_bytes=mib * 1024 * 1024)


def prepare_kernel(table, normed, w_query, w_key, w_value, pool, partial, held, first, rest, sems):
    slots = held.shape[0]
    per = slots // CHUNKS
    pairs = partial.shape[0]
    requests = pairs // 2
    wide = w_query.shape[1]
    head = w_key.shape[1]

    def fetch(c):
        part = pl.ds(c * per, per)
        return pltpu.make_async_copy(pool.at[part], held.at[part], sems.at[c])

    for c in range(CHUNKS):
        fetch(c).start()
    hidden = jnp.concatenate([normed[s].astype(jnp.float32) for s in range(STEPS)], 0).astype(jnp.bfloat16)
    start = 0
    for weight, width in ((w_query, wide), (w_key, head), (w_value, head)):
        result = jnp.dot(hidden, weight[...], preferred_element_type=jnp.float32)
        for p in range(pairs):
            for s in range(STEPS):
                row = s * requests + p % requests
                partial[p, s : s + 1, start : start + width] = result[row : row + 1]
        start += width
    for c in range(CHUNKS):
        fetch(c).wait()

    def sort_first(j, carry):
        first[j] = held[table[0, j]]
        return carry

    def sort_rest(j, carry):
        rest[j] = held[table[0, MOVED_MAX + j]]
        return carry

    lax.fori_loop(0, first.shape[0], sort_first, 0, unroll=8)
    lax.fori_loop(0, rest.shape[0], sort_rest, 0, unroll=8)


def prepare(table, normed, w_query, w_key, w_value, pool, pairs):
    page = pool.shape[1:]
    wide = w_query.shape[1] + 2 * w_key.shape[1]
    return pl.pallas_call(
        prepare_kernel,
        out_shape=(
            jax.ShapeDtypeStruct((pairs, STEPS, wide), jnp.float32),
            jax.ShapeDtypeStruct(pool.shape, pool.dtype),
            jax.ShapeDtypeStruct((MOVED_MAX,) + page, pool.dtype),
            jax.ShapeDtypeStruct((PAGES_HALF - MOVED_MAX,) + page, pool.dtype),
        ),
        in_specs=[SMEM, VMEM, VMEM, VMEM, VMEM, HBM],
        out_specs=(VMEM, VMEM, VMEM, VMEM),
        scratch_shapes=[pltpu.SemaphoreType.DMA((CHUNKS,))],
        compiler_params=params(32),
        name="prepare",
    )(table, normed, w_query, w_key, w_value, pool)


def attention_kernel(lengths, sums, b_query, b_key, b_value, cosine, sine, first, rest, packed, entries, score):
    requests = sums.shape[0] // 2
    page_len = first.shape[1]
    group, head = b_query.shape
    rows = STEPS * group
    pair_index = lax.axis_index("pair")
    is_source = pair_index >= requests
    request = jnp.where(is_source, pair_index - requests, pair_index)
    half_tokens = PAGES_HALF * page_len
    limit = jnp.where(is_source, lengths[request] - half_tokens, half_tokens)

    total = sums[0]
    for p in range(1, sums.shape[0]):
        total = total + sums[p]
    query = jnp.concatenate(
        [total[s : s + 1, h * head : (h + 1) * head] for s in range(STEPS) for h in range(group)], 0
    )
    query = query + jnp.concatenate([b_query[...]] * STEPS, 0)
    cos_new = cosine[request]
    sin_new = sine[request]
    row = lax.broadcasted_iota(jnp.int32, (rows, head), 0)
    cos_rows = jnp.where(row < group, cos_new[0:1], cos_new[1:2])
    sin_rows = jnp.where(row < group, sin_new[0:1], sin_new[1:2])
    query = (query * cos_rows + pltpu.roll(query, head // 2, 1) * sin_rows).astype(jnp.bfloat16)
    key_new = total[:, group * head : (group + 1) * head] + b_key[...]
    key_new = jnp.concatenate([key_new, jnp.zeros((8 - STEPS, head), jnp.float32)], 0)
    key_new = key_new * cos_new + pltpu.roll(key_new, head // 2, 1) * sin_new
    key_new = key_new.astype(jnp.bfloat16).astype(jnp.float32)
    value_new = total[:, (group + 1) * head :] + b_value[...]
    value_new = value_new.astype(jnp.bfloat16).astype(jnp.float32)
    entries[:, :head] = key_new
    entries[0:STEPS, head:] = value_new
    entries[STEPS:, head:] = jnp.zeros((8 - STEPS, head), jnp.float32)
    scale = 1.0 / math.sqrt(head)

    column = lax.broadcasted_iota(jnp.int32, (rows, 1), 0)
    query_wide = query.astype(jnp.float32)
    fresh = []
    for s in range(STEPS):
        dots = jnp.sum(query_wide * key_new[s : s + 1], 1, keepdims=True) * scale
        seen = jnp.logical_and(is_source, column >= s * group)
        fresh.append((jnp.where(seen, dots, NEG), seen))
    row_max = jnp.maximum(fresh[0][0], fresh[1][0])

    per = 64
    width = per * page_len
    blocks = [(ref, i, i + per) for ref in (first, rest) for i in range(0, ref.shape[0], per)]
    lane = lax.broadcasted_iota(jnp.int32, (rows, width), 1)
    for c, (ref, low, high) in enumerate(blocks):
        keys = ref[low:high, :, :head].reshape(width, head)
        part = lax.dot_general(query, keys, (((1,), (1,)), ((), ())), preferred_element_type=jnp.float32)
        part = jnp.where(lane < limit - c * width, part * scale, NEG)
        score[:, c * width : (c + 1) * width] = part
        row_max = jnp.maximum(row_max, jnp.max(part, 1, keepdims=True))
    row_sum = jnp.zeros((rows, 1), jnp.float32)
    out = jnp.zeros((rows, head), jnp.float32)
    for s in range(STEPS):
        weight = jnp.where(fresh[s][1], jnp.exp(fresh[s][0] - row_max), 0.0)
        row_sum = row_sum + weight
        out = out + weight.astype(jnp.bfloat16).astype(jnp.float32) * value_new[s : s + 1]
    for c, (ref, low, high) in enumerate(blocks):
        weight = jnp.exp(score[:, c * width : (c + 1) * width] - row_max)
        weight = jnp.where(lane < limit - c * width, weight, 0.0)
        row_sum = row_sum + jnp.sum(weight, 1, keepdims=True)
        values = ref[low:high, :, head:].reshape(width, head)
        out = out + jnp.dot(weight.astype(jnp.bfloat16), values, preferred_element_type=jnp.float32)

    diagonal = lax.broadcasted_iota(jnp.int32, (rows, head), 1) == row
    packed[0:rows] = out
    packed[rows : rows + 1] = jnp.sum(jnp.where(diagonal, row_max, 0.0), 0, keepdims=True)
    packed[rows + 1 : rows + 2] = jnp.sum(jnp.where(diagonal, row_sum, 0.0), 0, keepdims=True)
    packed[rows + 2 :] = jnp.zeros((packed.shape[0] - rows - 2, head), jnp.float32)


def attend(lengths, sums, b_query, b_key, b_value, cosine, sine, first, rest):
    group, head = b_query.shape
    rows = STEPS * group
    tokens = PAGES_HALF * first.shape[1]
    return pl.pallas_call(
        attention_kernel,
        out_shape=(
            jax.ShapeDtypeStruct((rows + 8, head), jnp.float32),
            jax.ShapeDtypeStruct((8, 2 * head), jnp.float32),
        ),
        in_specs=[SMEM] + [VMEM] * 8,
        out_specs=(VMEM, VMEM),
        scratch_shapes=[pltpu.VMEM((rows, tokens), jnp.float32)],
        compiler_params=params(24),
        name="attend",
    )(lengths, sums, b_query, b_key, b_value, cosine, sine, first, rest)


def project_kernel(parts, w_out, out):
    pairs, packed_rows, head = parts.shape
    rows = packed_rows - 8
    group = rows // STEPS
    requests = pairs // 2
    lane = lax.broadcasted_iota(jnp.int32, (rows, head), 1)
    diagonal = lane == lax.broadcasted_iota(jnp.int32, (rows, head), 0)

    def as_column(line):
        return jnp.sum(jnp.where(diagonal, line, 0.0), 1, keepdims=True)

    merged = []
    for r in range(requests):
        first_max, first_sum = (as_column(parts[r, rows + i : rows + i + 1]) for i in range(2))
        second_max, second_sum = (as_column(parts[r + requests, rows + i : rows + i + 1]) for i in range(2))
        top = jnp.maximum(first_max, second_max)
        first_weight = jnp.exp(first_max - top)
        second_weight = jnp.exp(second_max - top)
        joined = first_weight * parts[r, :rows] + second_weight * parts[r + requests, :rows]
        merged.append(joined / (first_weight * first_sum + second_weight * second_sum))
    lines = []
    for s in range(STEPS):
        for r in range(requests):
            lines.append(
                jnp.concatenate(
                    [merged[r][s * group + h : s * group + h + 1] for h in range(group)], 1
                )
            )
    attended = jnp.concatenate(lines, 0).astype(jnp.bfloat16)
    out[...] = jnp.dot(attended, w_out[...], preferred_element_type=jnp.float32)


def project(parts, w_out):
    return pl.pallas_call(
        project_kernel,
        out_shape=jax.ShapeDtypeStruct((STEPS * parts.shape[0] // 2, w_out.shape[1]), jnp.float32),
        in_specs=[VMEM, VMEM],
        out_specs=VMEM,
        compiler_params=params(16),
        name="project",
    )(parts, w_out)


def finish_kernel(table, lengths, plan, entries, pages, held_in, held, new_pool, sems):
    del held_in
    slots, page_len, width = held.shape
    requests = lengths.shape[0]
    pair_index = lax.axis_index("pair")
    is_source = pair_index >= requests

    @pl.when(is_source)
    def _():
        page_row = lax.broadcasted_iota(jnp.int32, (page_len, width), 0)
        first_new = lengths[pair_index - requests] - PAGES_HALF * page_len
        for s in range(STEPS):
            offset = first_new + s
            slot = table[0, offset // page_len]
            old = held[slot].astype(jnp.float32)
            held[slot] = jnp.where(page_row == offset % page_len, entries[s : s + 1], old).astype(held.dtype)

    @pl.when(jnp.logical_not(is_source))
    def _():
        def place(j, carry):
            held[table[0, PAGES_HALF + j]] = pages[j]
            return carry

        count = plan[pair_index, 0]
        for s in range(1, STEPS):
            count = count + plan[pair_index, s]
        lax.fori_loop(0, count, place, 0)

    per = slots // CHUNKS

    def store(c):
        part = pl.ds(c * per, per)
        return pltpu.make_async_copy(held.at[part], new_pool.at[part], sems.at[c])

    for c in range(CHUNKS):
        store(c).start()
    for c in range(CHUNKS):
        store(c).wait()


def finish(table, lengths, plan, entries, pages, held):
    return pl.pallas_call(
        finish_kernel,
        out_shape=(
            jax.ShapeDtypeStruct(held.shape, held.dtype),
            jax.ShapeDtypeStruct(held.shape, held.dtype),
        ),
        in_specs=[SMEM, SMEM, SMEM, VMEM, VMEM, VMEM],
        out_specs=(VMEM, HBM),
        scratch_shapes=[pltpu.SemaphoreType.DMA((CHUNKS,))],
        input_output_aliases={5: 0},
        compiler_params=params(24),
        name="finish",
    )(table, lengths, plan, entries, pages, held)[1]


def local(
    normed, w_query, b_query, w_key, b_key, w_value, b_value, w_out, pool, page_table, lengths, plan
):
    pair_count = lax.axis_size("pair")
    tp_count = lax.axis_size("tp")
    requests = pair_count // 2
    head = w_key.shape[1]

    partial, held, first, rest = prepare(
        page_table, normed, w_query, w_key, w_value, pool[0, 0], pair_count
    )
    route = [(i + requests, i) for i in range(requests)]
    incoming = lax.ppermute(first, "pair", route)
    sums = lax.all_to_all(partial, "pair", split_axis=0, concat_axis=0, tiled=True)

    frequency = rope_base ** (-(jnp.arange(head // 2, dtype=jnp.float32) * 2.0 / head))
    steps = jnp.minimum(jnp.arange(8, dtype=jnp.int32), STEPS - 1)
    position = (lengths[:, None] + steps[None, :]).astype(jnp.float32)[..., None]
    angles = position * frequency
    cosine = jnp.cos(angles)
    sine = jnp.sin(angles)
    cosine = jnp.concatenate([cosine, cosine], -1)
    sine = jnp.concatenate([-sine, sine], -1)

    packed, entries = attend(
        lengths,
        sums,
        b_query.reshape(-1, head),
        b_key[None, :],
        b_value[None, :],
        cosine,
        sine,
        first,
        rest,
    )
    spread = jnp.broadcast_to(packed[None], (pair_count,) + packed.shape)
    parts = lax.all_to_all(spread, "pair", split_axis=0, concat_axis=0, tiled=True)
    projected = project(parts, w_out)
    if tp_count == 2:
        projected = projected + lax.ppermute(projected, "tp", [(0, 1), (1, 0)])
    else:
        projected = lax.psum(projected, "tp")
    attended = projected.reshape(STEPS, requests, w_out.shape[1])
    new_pool = finish(page_table, lengths, plan, entries, incoming, held)
    return attended, new_pool[None, None]


def solution(mesh):
    return jax.shard_map(
        local,
        mesh=mesh,
        in_specs=(
            P(None, "rep", "pair"),
            P("pair", "tp"),
            P("tp"),
            P("pair", "tp"),
            P("tp"),
            P("pair", "tp"),
            P("tp"),
            P("tp", "pair"),
            P(("rep", "pair"), "tp", None, None, None),
            P(("rep", "pair"), None),
            P("rep"),
            P("rep", None),
        ),
        out_specs=(P(None, "rep", "pair"), P(("rep", "pair"), "tp", None, None, None)),
        check_vma=False,
    )
```

profile of v0, /device:TPU:0, one launch (start us, length us, event | category | flops | bytes accessed | tf_op | source)
XLA Modules:
  0.0 91.6 jit_solution(18049883069000751518)
XLA Ops:
  0.6 0.0 copy-start.12
  0.6 0.0 copy-start.15
  0.7 0.0 copy-start.14
  0.7 0.0 copy-start
  0.7 2.2 %copy-done = bf16[1,1,512,16,256]{4,3,2,1,0:T(8,128)(2,1)S(1)} copy-done((bf16[1,1,512,16,256]{4,3,2,1,0:T(8,128)(2,1)S(1)}, bf16[1,1,512,16,256]{4,3,2,1,0:T(8,128)(2,1)}, u32[]{:S(2)}) %copy-start) | copy-done | bytes 4194328
  2.9 0.0 copy-start.3
  2.9 1.6 %copy-done.3 = bf16[1024,1024]{1,0:T(8,128)(2,1)S(1)} copy-done((bf16[1024,1024]{1,0:T(8,128)(2,1)S(1)}, bf16[1024,1024]{1,0:T(8,128)(2,1)}, u32[]{:S(2)}) %copy-start.3) | copy-done | bytes 2097176
  4.5 0.0 copy-start.7
  4.5 0.9 %copy-done.7 = bf16[1024,128]{1,0:T(8,128)(2,1)S(1)} copy-done((bf16[1024,128]{1,0:T(8,128)(2,1)S(1)}, bf16[1024,128]{1,0:T(8,128)(2,1)}, u32[]{:S(2)}) %copy-start.7) | copy-done | bytes 262168
  5.4 0.0 copy-start.8
  5.4 0.9 %copy-done.8 = bf16[1024,128]{1,0:T(8,128)(2,1)S(1)} copy-done((bf16[1024,128]{1,0:T(8,128)(2,1)S(1)}, bf16[1024,128]{1,0:T(8,128)(2,1)}, u32[]{:S(2)}) %copy-start.8) | copy-done | bytes 262168
  6.4 0.0 copy-start.9
  6.4 0.7 copy-done.9
  7.1 0.0 copy-start.10
  7.1 0.7 copy-done.10
  7.8 0.0 copy-start.13
  7.8 0.0 copy-start.4
  7.8 2.7 %prepare.1 = (f32[8,2,1280]{2,1,0:T(2,128)}, bf16[512,16,256]{2,1,0:T(8,128)(2,1)S(1)}, bf16[128,16,256]{2,1,0:T(8,128)(2,1)S(1)}, bf16[256,16,256]{2,1,0:T(8,128)(2,1)S(1)}) custom-call(s32[1,512]{1,0:T(1,128)S(1)} %copy-done.10, bf16[2,4,1024]{2,1,0:T(4,128)(2,1)S(1)} %copy-done.9, bf16[1024,1024]{1,0:T(8,128)(2,1)S(1)} %copy-done.3, ...), custom_call_target="tpu_custom_call" | custom-call | tf_op jit(solution)/shard_map/prepare/pallas_call | solution.py:69
  10.5 0.0 copy-start.1
  10.5 2.0 %copy-done.1 = bf16[512,16,256]{2,1,0:T(8,128)(2,1)} copy-done((bf16[512,16,256]{2,1,0:T(8,128)(2,1)}, bf16[512,16,256]{2,1,0:T(8,128)(2,1)S(1)}, u32[]{:S(2)}) %copy-start.1) | copy-done | bytes 4194328
  12.5 0.0 copy-start.5
  12.5 1.3 %copy-done.5 = bf16[256,16,256]{2,1,0:T(8,128)(2,1)} copy-done((bf16[256,16,256]{2,1,0:T(8,128)(2,1)}, bf16[256,16,256]{2,1,0:T(8,128)(2,1)S(1)}, u32[]{:S(2)}) %copy-start.5) | copy-done | bytes 2097176
  13.9 0.0 copy-start.16
  13.9 0.0 copy-start.11
  13.9 1.4 %collective-permute-start.1 = (bf16[128,16,256]{2,1,0:T(8,128)(2,1)S(1)}, bf16[128,16,256]{2,1,0:T(8,128)(2,1)}, u32[]{:S(2)}, u32[]{:S(2)}) collective-permute-start(bf16[128,16,256]{2,1,0:T(8,128)(2,1)S(1)} %get-tuple-element.10.first), channel_id=1, source_target_pairs={{16,0},{20,4},{24,8},{28,12},{17,1},{21,5},{25,9},{29,13},{18,2},{... | collective-permute-start | bytes 3145736 | tf_op jit(solution)/shard_map/ppermute | solution.py:288
  15.3 9.2 %all-to-all-start = ((f32[8,2,1280]{2,1,0:T(2,128)}), f32[8,2,1280]{2,1,0:T(2,128)S(1)}, u32[]{:S(2)}, u32[]{:S(2)}) async-start(f32[8,2,1280]{2,1,0:T(2,128)} %get-tuple-element.9), calls=%async_computation | async-start | bytes 163840 | tf_op jit(solution)/shard_map/all_to_all | solution.py:289
  24.5 0.0 copy-done.12
  24.5 0.1 add_convert_fusion
  24.6 0.1 fusion
  24.7 0.1 pad_maximum_fusion
  24.8 43.1 %all-to-all-done.sums = f32[8,2,1280]{2,1,0:T(2,128)S(1)} async-done(((f32[8,2,1280]{2,1,0:T(2,128)}), f32[8,2,1280]{2,1,0:T(2,128)S(1)}, u32[]{:S(2)}, u32[]{:S(2)}) %all-to-all-start) | async-done | bytes 81952 | tf_op jit(solution)/shard_map/all_to_all | solution.py:289
  67.9 0.0 copy-done.15
  67.9 0.0 copy-done.14
  68.0 0.0 copy-done.13
  68.0 0.0 copy-start.6
  68.0 1.6 %copy-done.6 = bf16[256,16,256]{2,1,0:T(8,128)(2,1)S(1)} copy-done((bf16[256,16,256]{2,1,0:T(8,128)(2,1)S(1)}, bf16[256,16,256]{2,1,0:T(8,128)(2,1)}, u32[]{:S(2)}) %copy-start.6) | copy-done | bytes 2097176
  69.5 1.5 %attend.1 = (f32[24,128]{1,0:T(8,128)S(1)}, f32[8,256]{1,0:T(8,128)S(1)}) custom-call(s32[4]{0:T(128)S(1)} %copy-done.12, f32[8,2,1280]{2,1,0:T(2,128)S(1)} %all-to-all-done.sums, f32[8,128]{1,0:T(8,128)S(1)} %bitcast.6, f32[1,128]{1,0:T(1,128)S(1)} %bitcast.7, f32[1,128]{1,0:T(1,128)S(1)} %bitcast.8, f32[4,8,128]{2,1,0:T(8,128)S(1)} %get-tuple-element.19.cosine, ...), custom_call_target="tpu_custom_call" | custom-call | tf_op jit(solution)/shard_map/attend/pallas_call | solution.py:163
  71.1 9.5 %all_to_all.10.parts = f32[8,24,128]{2,1,0:T(8,128)S(1)} all-to-all(f32[8,24,128]{2,1,0:T(8,128)S(1)} %broadcast_in_dim.10), channel_id=1, replica_groups=mesh['pair'=8,'tp'=2,'rep'=2] {'pair'}, dimensions={0} | all-to-all | bytes 196608 | tf_op jit(solution)/shard_map/all_to_all | solution.py:312
  80.6 0.0 copy-done.4
  80.6 0.5 project.1
  81.1 1.5 %collective-permute-start = (f32[8,1024]{1,0:T(8,128)S(1)}, f32[8,1024]{1,0:T(8,128)S(1)}, u32[]{:S(2)}, u32[]{:S(2)}) collective-permute-start(f32[8,1024]{1,0:T(8,128)S(1)} %project.1), channel_id=1, source_target_pairs={{0,2},{2,0},{1,3},{3,1},{4,6},{6,4},{5,7},{7,5},{8,10},{10,8},{9,1... | collective-permute-start | bytes 98312 | tf_op jit(solution)/shard_map/ppermute | solution.py:315
  82.6 0.0 copy-done.16
  82.6 0.1 copy.15.plan
  82.7 2.3 %collective-permute-done = f32[8,1024]{1,0:T(8,128)S(1)} collective-permute-done((f32[8,1024]{1,0:T(8,128)S(1)}, f32[8,1024]{1,0:T(8,128)S(1)}, u32[]{:S(2)}, u32[]{:S(2)}) %collective-permute-start) | collective-permute-done | bytes 32800 | tf_op jit(solution)/shard_map/ppermute | solution.py:315
  85.0 0.6 reshape.51
  85.7 0.0 collective-permute-done.1.pages
  85.7 0.0 copy-done.11
  85.7 0.0 copy-start.2
  85.7 2.2 %copy-done.2 = bf16[512,16,256]{2,1,0:T(8,128)(2,1)S(1)} copy-done((bf16[512,16,256]{2,1,0:T(8,128)(2,1)S(1)}, bf16[512,16,256]{2,1,0:T(8,128)(2,1)}, u32[]{:S(2)}) %copy-start.2) | copy-done | bytes 4194328
  87.9 3.7 %finish.1 = (bf16[512,16,256]{2,1,0:T(8,128)(2,1)S(1)}, bf16[512,16,256]{2,1,0:T(8,128)(2,1)}) custom-call(s32[1,512]{1,0:T(1,128)S(1)} %copy-done.11, s32[4]{0:T(128)S(1)} %copy-done.12, s32[4,2]{1,0:T(4,128)S(1)} %copy.15.plan, f32[8,256]{1,0:T(8,128)S(1)} %get-tuple-element.13.entries, ...), custom_call_target="tpu_custom_call", output_to_operand_aliasing={{0}: (5, {})} | custom-call | tf_op jit(solution)/shard_map/finish/pallas_call | solution.py:261
  (4 shorter events, 0.0 us)
Async XLA Ops:
  0.6 23.9 %copy-start.12 = (s32[4]{0:T(128)S(1)}, s32[4]{0:T(128)}, u32[]{:S(2)}) copy-start(s32[4]{0:T(128)} %lengths.3) | copy-start | bytes 52
  0.6 67.3 %copy-start.15 = (f32[128]{0:T(128)S(1)}, f32[128]{0:T(128)}, u32[]{:S(2)}) copy-start(f32[128]{0:T(128)} %param.18) | copy-start | bytes 1540
  0.7 67.3 %copy-start.14 = (f32[128]{0:T(128)S(1)}, f32[128]{0:T(128)}, u32[]{:S(2)}) copy-start(f32[128]{0:T(128)} %param.16) | copy-start | bytes 1540
  0.7 2.2 %copy-start = (bf16[1,1,512,16,256]{4,3,2,1,0:T(8,128)(2,1)S(1)}, bf16[1,1,512,16,256]{4,3,2,1,0:T(8,128)(2,1)}, u32[]{:S(2)}) copy-start(bf16[1,1,512,16,256]{4,3,2,1,0:T(8,128)(2,1)} %param.20) | copy-start | bytes 12582916
  2.9 1.6 %copy-start.3 = (bf16[1024,1024]{1,0:T(8,128)(2,1)S(1)}, bf16[1024,1024]{1,0:T(8,128)(2,1)}, u32[]{:S(2)}) copy-start(bf16[1024,1024]{1,0:T(8,128)(2,1)} %w_query.1) | copy-start | bytes 6291460
  4.5 0.9 %copy-start.7 = (bf16[1024,128]{1,0:T(8,128)(2,1)S(1)}, bf16[1024,128]{1,0:T(8,128)(2,1)}, u32[]{:S(2)}) copy-start(bf16[1024,128]{1,0:T(8,128)(2,1)} %w_key.1) | copy-start | bytes 786436
  5.4 0.9 %copy-start.8 = (bf16[1024,128]{1,0:T(8,128)(2,1)S(1)}, bf16[1024,128]{1,0:T(8,128)(2,1)}, u32[]{:S(2)}) copy-start(bf16[1024,128]{1,0:T(8,128)(2,1)} %w_value.1) | copy-start | bytes 786436
  6.4 0.7 copy-start.9
  7.1 0.7 copy-start.10
  7.8 60.2 %copy-start.13 = (f32[1024]{0:T(1024)S(1)}, f32[1024]{0:T(1024)}, u32[]{:S(2)}) copy-start(f32[1024]{0:T(1024)} %param.14) | copy-start | bytes 12292
  7.8 72.9 %copy-start.4 = (bf16[1024,1024]{1,0:T(8,128)(2,1)S(1)}, bf16[1024,1024]{1,0:T(8,128)(2,1)}, u32[]{:S(2)}) copy-start(bf16[1024,1024]{1,0:T(8,128)(2,1)} %w_out.1) | copy-start | bytes 6291460
  10.5 2.0 %copy-start.1 = (bf16[512,16,256]{2,1,0:T(8,128)(2,1)}, bf16[512,16,256]{2,1,0:T(8,128)(2,1)S(1)}, u32[]{:S(2)}) copy-start(bf16[512,16,256]{2,1,0:T(8,128)(2,1)S(1)} %get-tuple-element.14.held_in) | copy-start | bytes 12582916
  12.5 1.3 %copy-start.5 = (bf16[256,16,256]{2,1,0:T(8,128)(2,1)}, bf16[256,16,256]{2,1,0:T(8,128)(2,1)S(1)}, u32[]{:S(2)}) copy-start(bf16[256,16,256]{2,1,0:T(8,128)(2,1)S(1)} %get-tuple-element.11.rest) | copy-start | bytes 6291460
  13.9 68.8 %copy-start.16 = (s32[4,2]{0,1:T(2,128)S(1)}, s32[4,2]{0,1:T(2,128)}, u32[]{:S(2)}) copy-start(s32[4,2]{0,1:T(2,128)} %param.23) | copy-start | bytes 100
  13.9 71.8 %copy-start.11 = (s32[1,512]{1,0:T(1,128)S(1)}, s32[1,512]{1,0:T(1,128)}, u32[]{:S(2)}) copy-start(s32[1,512]{1,0:T(1,128)} %table.3) | copy-start | bytes 6148
  13.9 71.8 %collective-permute-start.1 = (bf16[128,16,256]{2,1,0:T(8,128)(2,1)S(1)}, bf16[128,16,256]{2,1,0:T(8,128)(2,1)}, u32[]{:S(2)}, u32[]{:S(2)}) collective-permute-start(bf16[128,16,256]{2,1,0:T(8,128)(2,1)S(1)} %get-tuple-element.10.first), channel_id=1, source_target_pairs={{16,0},{20,4},{24,8},{28,12},{17,1},{21,5},{25,9},{29,13},{18,2},{... | collective-permute-start | bytes 3145736 | tf_op jit(solution)/shard_map/ppermute | solution.py:288
  15.3 52.7 %all-to-all-start = ((f32[8,2,1280]{2,1,0:T(2,128)}), f32[8,2,1280]{2,1,0:T(2,128)S(1)}, u32[]{:S(2)}, u32[]{:S(2)}) async-start(f32[8,2,1280]{2,1,0:T(2,128)} %get-tuple-element.9), calls=%async_computation | async-start | bytes 163840 | tf_op jit(solution)/shard_map/all_to_all | solution.py:289
  68.0 1.6 %copy-start.6 = (bf16[256,16,256]{2,1,0:T(8,128)(2,1)S(1)}, bf16[256,16,256]{2,1,0:T(8,128)(2,1)}, u32[]{:S(2)}) copy-start(bf16[256,16,256]{2,1,0:T(8,128)(2,1)} %copy-done.5) | copy-start | bytes 6291460
  81.1 3.9 %collective-permute-start = (f32[8,1024]{1,0:T(8,128)S(1)}, f32[8,1024]{1,0:T(8,128)S(1)}, u32[]{:S(2)}, u32[]{:S(2)}) collective-permute-start(f32[8,1024]{1,0:T(8,128)S(1)} %project.1), channel_id=1, source_target_pairs={{0,2},{2,0},{1,3},{3,1},{4,6},{6,4},{5,7},{7,5},{8,10},{10,8},{9,1... | collective-permute-start | bytes 98312 | tf_op jit(solution)/shard_map/ppermute | solution.py:315
  85.7 2.2 %copy-start.2 = (bf16[512,16,256]{2,1,0:T(8,128)(2,1)S(1)}, bf16[512,16,256]{2,1,0:T(8,128)(2,1)}, u32[]{:S(2)}) copy-start(bf16[512,16,256]{2,1,0:T(8,128)(2,1)} %copy-done.1) | copy-start | bytes 12582916
where the time goes:
time: 92.2 us; the launch traced here: 91.6 us
  waiting for transfers between devices  45.4 us (49%)
  local copies, waits for them, and re-layouts  15 us (16%)
  starting transfers between devices  12.1 us (13%)
  blocking collectives  9.51 us (10%)
  Pallas kernels  8.49 us (9%)
    all_to_all x1, waiting for transfers between devices, local(): lax.all_to_all(partial, 'pair', split_axis=0, concat_axis=0, tiled=True)  43.1 us
    unnamed x35, local copies, waits for them, and re-layouts  14.3 us
    all_to_all x1, blocking collectives, local(): lax.all_to_all(spread, 'pair', split_axis=0, concat_axis=0, tiled=True)  9.51 us
    all_to_all x1, starting transfers between devices, local(): lax.all_to_all(partial, 'pair', split_axis=0, concat_axis=0, tiled=True)  9.19 us
    pallas_call x1, Pallas kernels, finish(): pl.pallas_call(finish_kernel, out_shape=(jax.ShapeDtypeStruct(held.shape,...  3.74 us
    pallas_call x1, Pallas kernels, prepare(): pl.pallas_call(prepare_kernel, out_shape=(jax.ShapeDtypeStruct((pairs, ST...  2.73 us
    ppermute x1, waiting for transfers between devices, local(): projected = projected + lax.ppermute(projected, 'tp', [(0, 1), (1, 0)])  2.3 us
  transfers between devices with their start and end apart: 3, of which 2 were waited for; matrix products, arithmetic and copies ran while one was open for 1% of the time, Pallas kernels for 2%

commit v1 on v0

--- a/solution.py
+++ b/solution.py
@@ -11,6 +11,8 @@
 STEPS = 2
 SECTION = 64
 MOVED_MAX = STEPS * SECTION
+PIECES = (16, 16, 96, 128, 128)
+MOVED_PIECES = 3
 CHUNKS = 8
 NEG = -1e30
 
@@ -21,46 +23,64 @@
 HBM = pl.BlockSpec(memory_space=pltpu.HBM)
 
 
+def in_hbm(*arrays):
+    return tuple(pltpu.with_memory_space_constraint(a, pltpu.HBM) for a in arrays)
+
+
 def params(mib):
     return pltpu.CompilerParams(vmem_limit_bytes=mib * 1024 * 1024)
 
 
-def prepare_kernel(table, normed, w_query, w_key, w_value, pool, partial, held, first, rest, sems):
+def prepare_kernel(
+    table, normed, w_query, w_key, w_value, pool, partial, *refs
+):
+    pieces, (held, order, w_all, sems, out_sems, w_sems) = refs[: len(refs) - 6], refs[len(refs) - 6 :]
     slots = held.shape[0]
     per = slots // CHUNKS
     pairs = partial.shape[0]
     requests = pairs // 2
-    wide = w_query.shape[1]
     head = w_key.shape[1]
+
+    weights = []
+    start = 0
+    for i, weight in enumerate((w_query, w_key, w_value)):
+        part = w_all.at[:, start : start + weight.shape[1]]
+        weights.append(pltpu.make_async_copy(weight, part, w_sems.at[i]))
+        start += weight.shape[1]
 
     def fetch(c):
         part = pl.ds(c * per, per)
         return pltpu.make_async_copy(pool.at[part], held.at[part], sems.at[c])
 
+    for copy in weights:
+        copy.start()
     for c in range(CHUNKS):
         fetch(c).start()
     hidden = jnp.concatenate([normed[s].astype(jnp.float32) for s in range(STEPS)], 0).astype(jnp.bfloat16)
-    start = 0
-    for weight, width in ((w_query, wide), (w_key, head), (w_value, head)):
-        result = jnp.dot(hidden, weight[...], preferred_element_type=jnp.float32)
-        for p in range(pairs):
-            for s in range(STEPS):
-                row = s * requests + p % requests
-                partial[p, s : s + 1, start : start + width] = result[row : row + 1]
-        start += width
+    for copy in weights:
+        copy.wait()
+    result = jnp.dot(hidden, w_all[...], preferred_element_type=jnp.float32)
+    for p in range(pairs):
+        for s in range(STEPS):
+            row = s * requests + p % requests
+            partial[p, s : s + 1] = result[row : row + 1]
     for c in range(CHUNKS):
         fetch(c).wait()
 
-    def sort_first(j, carry):
-        first[j] = held[table[0, j]]
+    def sort(j, carry):
+        order[j] = held[table[0, j]]
         return carry
 
-    def sort_rest(j, carry):
-        rest[j] = held[table[0, MOVED_MAX + j]]
-        return carry
-
-    lax.fori_loop(0, first.shape[0], sort_first, 0, unroll=8)
-    lax.fori_loop(0, rest.shape[0], sort_rest, 0, unroll=8)
+    copies = []
+    low = 0
+    for i, piece in enumerate(pieces):
+        high = low + piece.shape[0]
+        lax.fori_loop(low, high, sort, 0, unroll=8)
+        copies.append(pltpu.make_async_copy(order.at[pl.ds(low, piece.shape[0])], piece, out_sems.at[i]))
+        copies[-1].start()
+        low = high
+    for copy in copies:
+        copy.wait()
 
 
 def prepare(table, normed, w_query, w_key, w_value, pool, pairs):
@@ -68,23 +88,34 @@
     wide = w_query.shape[1] + 2 * w_key.shape[1]
     return pl.pallas_call(
         prepare_kernel,
-        out_shape=(
-            jax.ShapeDtypeStruct((pairs, STEPS, wide), jnp.float32),
-            jax.ShapeDtypeStruct(pool.shape, pool.dtype),
-            jax.ShapeDtypeStruct((MOVED_MAX,) + page, pool.dtype),
-            jax.ShapeDtypeStruct((PAGES_HALF - MOVED_MAX,) + page, pool.dtype),
-        ),
-        in_specs=[SMEM, VMEM, VMEM, VMEM, VMEM, HBM],
-        out_specs=(VMEM, VMEM, VMEM, VMEM),
-        scratch_shapes=[pltpu.SemaphoreType.DMA((CHUNKS,))],
-        compiler_params=params(32),
+        out_shape=(jax.ShapeDtypeStruct((pairs, STEPS, wide), jnp.float32),)
+        + tuple(pltpu.HBM((n,) + page, pool.dtype) for n in PIECES),
+        in_specs=[SMEM, VMEM, HBM, HBM, HBM, HBM],
+        out_specs=(VMEM,) + (HBM,) * len(PIECES),
+        scratch_shapes=[
+            pltpu.VMEM(pool.shape, pool.dtype),
+            pltpu.VMEM((PAGES_HALF,) + page, pool.dtype),
+            pltpu.VMEM((w_query.shape[0], wide), w_query.dtype),
+            pltpu.SemaphoreType.DMA((CHUNKS,)),
+            pltpu.SemaphoreType.DMA((len(PIECES),)),
+            pltpu.SemaphoreType.DMA((3,)),
+        ],
+        compiler_params=params(24),
         name="prepare",
-    )(table, normed, w_query, w_key, w_value, pool)
-
-
-def attention_kernel(lengths, sums, b_query, b_key, b_value, cosine, sine, first, rest, packed, entries, score):
+    )(table, normed, *in_hbm(w_query, w_key, w_value, pool))
+
+
+def attention_kernel(lengths, sums, b_query, b_key, b_value, cosine, sine, *refs):
+    pieces, (packed, entries, held, score, sems) = refs[: len(PIECES)], refs[len(PIECES) :]
+    copies = []
+    low = 0
+    for i, piece in enumerate(pieces):
+        size = piece.shape[0]
+        copies.append((low, pltpu.make_async_copy(piece, held.at[pl.ds(low, size)], sems.at[i])))
+        copies[-1][1].start()
+        low += size
     requests = sums.shape[0] // 2
-    page_len = first.shape[1]
+    page_len = held.shape[1]
     group, head = b_query.shape
     rows = STEPS * group
     pair_index = lax.axis_index("pair")
@@ -128,10 +159,13 @@
 
     per = 64
     width = per * page_len
-    blocks = [(ref, i, i + per) for ref in (first, rest) for i in range(0, ref.shape[0], per)]
+    blocks = PAGES_HALF // per
     lane = lax.broadcasted_iota(jnp.int32, (rows, width), 1)
-    for c, (ref, low, high) in enumerate(blocks):
-        keys = ref[low:high, :, :head].reshape(width, head)
+    for c in range(blocks):
+        low, high = c * per, (c + 1) * per
+        while copies and copies[0][0] < high:
+            copies.pop(0)[1].wait()
+        keys = held[low:high, :, :head].reshape(width, head)
         part = lax.dot_general(query, keys, (((1,), (1,)), ((), ())), preferred_element_type=jnp.float32)
         part = jnp.where(lane < limit - c * width, part * scale, NEG)
         score[:, c * width : (c + 1) * width] = part
@@ -142,11 +176,12 @@
         weight = jnp.where(fresh[s][1], jnp.exp(fresh[s][0] - row_max), 0.0)
         row_sum = row_sum + weight
         out = out + weight.astype(jnp.bfloat16).astype(jnp.float32) * value_new[s : s + 1]
-    for c, (ref, low, high) in enumerate(blocks):
+    for c in range(blocks):
+        low, high = c * per, (c + 1) * per
         weight = jnp.exp(score[:, c * width : (c + 1) * width] - row_max)
         weight = jnp.where(lane < limit - c * width, weight, 0.0)
         row_sum = row_sum + jnp.sum(weight, 1, keepdims=True)
-        values = ref[low:high, :, head:].reshape(width, head)
+        values = held[low:high, :, head:].reshape(width, head)
         out = out + jnp.dot(weight.astype(jnp.bfloat16), values, preferred_element_type=jnp.float32)
 
     diagonal = lax.broadcasted_iota(jnp.int32, (rows, head), 1) == row
@@ -156,22 +191,26 @@
     packed[rows + 2 :] = jnp.zeros((packed.shape[0] - rows - 2, head), jnp.float32)
 
 
-def attend(lengths, sums, b_query, b_key, b_value, cosine, sine, first, rest):
+def attend(lengths, sums, b_query, b_key, b_value, cosine, sine, pieces):
     group, head = b_query.shape
     rows = STEPS * group
-    tokens = PAGES_HALF * first.shape[1]
+    page = pieces[0].shape[1:]
     return pl.pallas_call(
         attention_kernel,
         out_shape=(
             jax.ShapeDtypeStruct((rows + 8, head), jnp.float32),
             jax.ShapeDtypeStruct((8, 2 * head), jnp.float32),
         ),
-        in_specs=[SMEM] + [VMEM] * 8,
+        in_specs=[SMEM] + [VMEM] * 6 + [HBM] * len(pieces),
         out_specs=(VMEM, VMEM),
-        scratch_shapes=[pltpu.VMEM((rows, tokens), jnp.float32)],
+        scratch_shapes=[
+            pltpu.VMEM((PAGES_HALF,) + page, pieces[0].dtype),
+            pltpu.VMEM((rows, PAGES_HALF * page[0]), jnp.float32),
+            pltpu.SemaphoreType.DMA((len(pieces),)),
+        ],
         compiler_params=params(24),
         name="attend",
-    )(lengths, sums, b_query, b_key, b_value, cosine, sine, first, rest)
+    )(lengths, sums, b_query, b_key, b_value, cosine, sine, *in_hbm(*pieces))
 
 
 def project_kernel(parts, w_out, out):
@@ -203,13 +242,15 @@
                 )
             )
     attended = jnp.concatenate(lines, 0).astype(jnp.bfloat16)
-    out[...] = jnp.dot(attended, w_out[...], preferred_element_type=jnp.float32)
+    result = jnp.dot(attended, w_out[...], preferred_element_type=jnp.float32)
+    for s in range(STEPS):
+        out[s] = result[s * requests : (s + 1) * requests]
 
 
 def project(parts, w_out):
     return pl.pallas_call(
         project_kernel,
-        out_shape=jax.ShapeDtypeStruct((STEPS * parts.shape[0] // 2, w_out.shape[1]), jnp.float32),
+        out_shape=jax.ShapeDtypeStruct((STEPS, parts.shape[0] // 2, w_out.shape[1]), jnp.float32),
         in_specs=[VMEM, VMEM],
         out_specs=VMEM,
         compiler_params=params(16),
@@ -217,12 +258,42 @@
     )(parts, w_out)
 
 
-def finish_kernel(table, lengths, plan, entries, pages, held_in, held, new_pool, sems):
-    del held_in
+def moved_pages(plan, request):
+    count = plan[request, 0]
+    for s in range(1, STEPS):
+        count = count + plan[request, s]
+    return count
+
+
+def copy_kernel(table, lengths, plan, entries, pool, *refs):
+    early, (new_pool, held, pages, sems, out_sems, page_sems) = refs[:-6], refs[-6:]
     slots, page_len, width = held.shape
+    per = slots // CHUNKS
     requests = lengths.shape[0]
     pair_index = lax.axis_index("pair")
     is_source = pair_index >= requests
+
+    def fetch(c):
+        part = pl.ds(c * per, per)
+        return pltpu.make_async_copy(pool.at[part], held.at[part], sems.at[c])
+
+    def store(c):
+        part = pl.ds(c * per, per)
+        return pltpu.make_async_copy(held.at[part], new_pool.at[part], out_sems.at[c])
+
+    for c in range(CHUNKS):
+        fetch(c).start()
+    copies = []
+    low = 0
+    for i, piece in enumerate(early):
+        size = piece.shape[0]
+        copies.append(pltpu.make_async_copy(piece, pages.at[pl.ds(low, size)], page_sems.at[i]))
+        copies[-1].start()
+        low += size
+    for copy in copies:
+        copy.wait()
+    for c in range(CHUNKS):
+        fetch(c).wait()
 
     @pl.when(is_source)
     def _():
@@ -240,16 +311,7 @@
             held[table[0, PAGES_HALF + j]] = pages[j]
             return carry
 
-        count = plan[pair_index, 0]
-        for s in range(1, STEPS):
-            count = count + plan[pair_index, s]
-        lax.fori_loop(0, count, place, 0)
-
-    per = slots // CHUNKS
-
-    def store(c):
-        part = pl.ds(c * per, per)
-        return pltpu.make_async_copy(held.at[part], new_pool.at[part], sems.at[c])
+        lax.fori_loop(0, jnp.minimum(moved_pages(plan, pair_index), pages.shape[0]), place, 0)
 
     for c in range(CHUNKS):
         store(c).start()
@@ -257,20 +319,56 @@
         store(c).wait()
 
 
-def finish(table, lengths, plan, entries, pages, held):
+def copy_pool(table, lengths, plan, entries, pool, early):
+    return pl.pallas_call(
+        copy_kernel,
+        out_shape=jax.ShapeDtypeStruct(pool.shape, pool.dtype),
+        in_specs=[SMEM, SMEM, SMEM, VMEM, HBM] + [HBM] * len(early),
+        out_specs=HBM,
+        scratch_shapes=[
+            pltpu.VMEM(pool.shape, pool.dtype),
+            pltpu.VMEM((sum(PIECES[: MOVED_PIECES - 1]),) + pool.shape[1:], pool.dtype),
+            pltpu.SemaphoreType.DMA((CHUNKS,)),
+            pltpu.SemaphoreType.DMA((CHUNKS,)),
+            pltpu.SemaphoreType.DMA((len(early),)),
+        ],
+        compiler_params=params(24),
+        name="copy_pool",
+    )(table, lengths, plan, entries, *in_hbm(pool, *early))
+
+
+def finish_kernel(table, plan, pages, base, new_pool, sem):
+    del base
+    requests = plan.shape[0]
+    pair_index = lax.axis_index("pair")
+    done = MOVED_MAX - pages.shape[0]
+    request = jnp.where(pair_index >= requests, 0, pair_index)
+    count = jnp.where(pair_index >= requests, 0, moved_pages(plan, request) - done)
+
+    def start(j, carry):
+        slot = table[0, PAGES_HALF + done + j]
+        pltpu.make_async_copy(pages.at[j], new_pool.at[slot], sem).start()
+        return carry
+
+    def wait(j, carry):
+        pltpu.make_async_copy(pages.at[0], new_pool.at[0], sem).wait()
+        return carry
+
+    lax.fori_loop(0, count, start, 0)
+    lax.fori_loop(0, count, wait, 0)
+
+
+def finish(table, plan, pages, base):
     return pl.pallas_call(
         finish_kernel,
-        out_shape=(
-            jax.ShapeDtypeStruct(held.shape, held.dtype),
-            jax.ShapeDtypeStruct(held.shape, held.dtype),
-        ),
-        in_specs=[SMEM, SMEM, SMEM, VMEM, VMEM, VMEM],
-        out_specs=(VMEM, HBM),
-        scratch_shapes=[pltpu.SemaphoreType.DMA((CHUNKS,))],
-        input_output_aliases={5: 0},
-        compiler_params=params(24),
+        out_shape=jax.ShapeDtypeStruct(base.shape, base.dtype),
+        in_specs=[SMEM, SMEM, VMEM, HBM],
+        out_specs=HBM,
+        scratch_shapes=[pltpu.SemaphoreType.DMA],
+        input_output_aliases={3: 0},
+        compiler_params=params(16),
         name="finish",
-    )(table, lengths, plan, entries, pages, held)[1]
+    )(table, plan, pages, base)
 
 
 def local(
@@ -281,12 +379,16 @@
     requests = pair_count // 2
     head = w_key.shape[1]
 
-    partial, held, first, rest = prepare(
-        page_table, normed, w_query, w_key, w_value, pool[0, 0], pair_count
-    )
+    partial, *pieces = prepare(page_table, normed, w_query, w_key, w_value, pool[0, 0], pair_count)
     route = [(i + requests, i) for i in range(requests)]
-    incoming = lax.ppermute(first, "pair", route)
+
+    def migrate(pages, after):
+        return lax.ppermute(lax.optimization_barrier((pages, after))[0], "pair", route)
+
+    incoming = [lax.ppermute(pieces[0], "pair", route)]
     sums = lax.all_to_all(partial, "pair", split_axis=0, concat_axis=0, tiled=True)
+    sums, incoming[0] = lax.optimization_barrier((sums, incoming[0]))
+    incoming.append(migrate(pieces[1], sums))
 
     frequency = rope_base ** (-(jnp.arange(head // 2, dtype=jnp.float32) * 2.0 / head))
     steps = jnp.minimum(jnp.arange(8, dtype=jnp.int32), STEPS - 1)
@@ -305,19 +407,20 @@
         b_value[None, :],
         cosine,
         sine,
-        first,
-        rest,
+        pieces,
     )
     spread = jnp.broadcast_to(packed[None], (pair_count,) + packed.shape)
     parts = lax.all_to_all(spread, "pair", split_axis=0, concat_axis=0, tiled=True)
+    parts, incoming[1] = lax.optimization_barrier((parts, incoming[1]))
+    incoming.append(migrate(pieces[2], parts))
+    new_pool = copy_pool(page_table, lengths, plan, entries, pool[0, 0], incoming[:-1])
     projected = project(parts, w_out)
     if tp_count == 2:
         projected = projected + lax.ppermute(projected, "tp", [(0, 1), (1, 0)])
     else:
         projected = lax.psum(projected, "tp")
-    attended = projected.reshape(STEPS, requests, w_out.shape[1])
-    new_pool = finish(page_table, lengths, plan, entries, incoming, held)
-    return attended, new_pool[None, None]
+    new_pool = finish(page_table, plan, incoming[-1], new_pool)
+    return projected, new_pool[None, None]
 
 
 def solution(mesh):

time: 92.2 us -> 83.3 us (0.903)
  local copies, waits for them, and re-layouts: 15 us -> 2.19 us
  blocking collectives: 9.51 us -> 0 us
  Pallas kernels: 8.49 us -> 16.9 us
  starting transfers between devices: 12.1 us -> 16 us
    ppermute x1 -> x3, waiting for transfers between devices: 0.01 us -> 46 us  [the longest x2 36.3 us: migrate(): lax.ppermute(lax.optimization_barrier((pages, after))[0], 'pair', route)]
    all_to_all x1, waiting for transfers between devices: 43.1 us -> 0.01 us  [local(): lax.all_to_all(partial, 'pair', split_axis=0, concat_axis=0, tiled=True)]
    unnamed x35 -> x23, local copies, waits for them, and re-layouts: 14.3 us -> 1.54 us
    all_to_all x1 -> x0, blocking collectives: 9.51 us -> none  [local(): lax.all_to_all(spread, 'pair', split_axis=0, concat_axis=0, tiled=True)]
    pallas_call x1, Pallas kernels: 2.73 us -> 6.44 us  [prepare(): pl.pallas_call(prepare_kernel, out_shape=(jax.ShapeDtypeStruct((pairs, ST...]
    all_to_all x0 -> x1, starting transfers between devices: none -> 3.36 us  [local(): lax.all_to_all(spread, 'pair', split_axis=0, concat_axis=0, tiled=True)]
    pallas_call x2 -> x3, Pallas kernels: 4.21 us -> 7.21 us  [the longest x1 5.16 us: copy_pool(): pl.pallas_call(copy_kernel, out_shape=jax.ShapeDtypeStruct(pool.shape, po...]
    ppermute x1 -> x3, starting transfers between devices: 1.41 us -> 3.85 us  [the longest x2 2.57 us: migrate(): lax.ppermute(lax.optimization_barrier((pages, after))[0], 'pair', route)]
  transfers between devices with their start and end apart: 3 -> 6, of which waited for: 2 -> 3; matrix products, arithmetic and copies ran while one was open for 1% -> 1% of each run, Pallas kernels for 2% -> 7%
where the time goes in v1:
time: 83.3 us; the launch traced here: 82.8 us
  waiting for transfers between devices  46 us (55%)
  Pallas kernels  16.9 us (20%)
  starting transfers between devices  16 us (19%)
  local copies, waits for them, and re-layouts  2.19 us (3%)
  other arithmetic  0.94 us (1%)
    ppermute x2, waiting for transfers between devices, migrate(): lax.ppermute(lax.optimization_barrier((pages, after))[0], 'pair', route)  36.3 us
    ppermute x1, waiting for transfers between devices, local(): incoming = [lax.ppermute(pieces[0], 'pair', route)]  9.68 us
    all_to_all x1, starting transfers between devices, local(): lax.all_to_all(partial, 'pair', split_axis=0, concat_axis=0, tiled=True)  7.26 us
    pallas_call x1, Pallas kernels, prepare(): pl.pallas_call(prepare_kernel, out_shape=(jax.ShapeDtypeStruct((pairs, ST...  6.44 us
    pallas_call x1, Pallas kernels, copy_pool(): pl.pallas_call(copy_kernel, out_shape=jax.ShapeDtypeStruct(pool.shape, po...  5.16 us
    all_to_all x1, starting transfers between devices, local(): lax.all_to_all(spread, 'pair', split_axis=0, concat_axis=0, tiled=True)  3.36 us
    pallas_call x1, Pallas kernels, attend(): pl.pallas_call(attention_kernel, out_shape=(jax.ShapeDtypeStruct((rows +...  3.22 us
    ppermute x2, starting transfers between devices, migrate(): lax.ppermute(lax.optimization_barrier((pages, after))[0], 'pair', route)  2.57 us
  transfers between devices with their start and end apart: 6, of which 3 were waited for; matrix products, arithmetic and copies ran while one was open for 1% of the time, Pallas kernels for 7%

profile of v1, /device:TPU:0, one launch (start us, length us, event | category | flops | bytes accessed | tf_op | source)
XLA Modules:
  0.0 82.8 jit_solution(2435833095001446910)
XLA Ops:
  0.6 0.0 copy-start.4
  0.6 0.0 copy-start.7
  0.7 0.0 copy-start.6
  0.7 0.0 copy-start.1
  0.7 0.7 copy-done.1
  1.4 0.0 copy-start.3
  1.4 0.7 copy-done.3
  2.1 0.0 copy-start.5
  2.1 0.0 copy-start
  2.1 6.4 %prepare.1 = (f32[8,2,1280]{2,1,0:T(2,128)}, bf16[16,16,256]{2,1,0:T(8,128)(2,1)}, bf16[16,16,256]{2,1,0:T(8,128)(2,1)}, bf16[96,16,256]{2,1,0:T(8,128)(2,1)}, b...) custom-call(s32[1,512]{1,0:T(1,128)S(1)} %copy-done.1, bf16[2,4,1024]{2,1,0:T(4,128)(2,1)S(1)} %copy-done.3, ...), custom_call_target="tpu_custom_call" | custom-call | tf_op jit(solution)/shard_map/prepare/pallas_call | solution.py:89
  8.5 0.0 copy-start.10
  8.5 0.0 copy-start.2
  8.6 7.3 %all-to-all-start = ((f32[8,2,1280]{2,1,0:T(2,128)}), f32[8,2,1280]{2,1,0:T(2,128)S(1)}, u32[]{:S(2)}, u32[]{:S(2)}) async-start(f32[8,2,1280]{2,1,0:T(2,128)} %get-tuple-element.16), calls=%async_computation | async-start | bytes 163840 | tf_op jit(solution)/shard_map/all_to_all | solution.py:389
  15.8 1.3 %collective-permute-start = (bf16[16,16,256]{2,1,0:T(8,128)(2,1)}, bf16[16,16,256]{2,1,0:T(8,128)(2,1)S(1)}, u32[]{:S(2)}, u32[]{:S(2)}) collective-permute-start(bf16[16,16,256]{2,1,0:T(8,128)(2,1)} %get-tuple-element.17.refs_0_), channel_id=1, source_target_pairs={{16,0},{20,4},{24,8},{28,12},{17,1},{21,5},{25,9},{29,13},{18,2},{... | collective-permute-start | bytes 393224 | tf_op jit(solution)/shard_map/ppermute | solution.py:388
  17.1 0.0 copy-done.4
  17.1 0.1 add_convert_fusion
  17.2 0.1 fusion
  17.4 0.1 pad_maximum_fusion
  17.4 9.7 %collective-permute-done.refs_0_ = bf16[16,16,256]{2,1,0:T(8,128)(2,1)S(1)} collective-permute-done((bf16[16,16,256]{2,1,0:T(8,128)(2,1)}, bf16[16,16,256]{2,1,0:T(8,128)(2,1)S(1)}, u32[]{:S(2)}, u32[]{:S(2)}) %collective-permute-start) | collective-permute-done | bytes 131104 | tf_op jit(solution)/shard_map/ppermute | solution.py:388
  27.1 0.0 copy-start.8
  27.1 0.0 all-to-all-done.sums
  27.1 0.0 copy-done.7
  27.1 0.0 copy-done.6
  27.1 0.0 copy-done.5
  27.2 3.2 %attend.1 = (f32[24,128]{1,0:T(8,128)S(1)}, f32[8,256]{1,0:T(8,128)S(1)}) custom-call(s32[4]{0:T(128)S(1)} %copy-done.4, f32[8,2,1280]{2,1,0:T(2,128)S(1)} %all-to-all-done.sums, f32[8,128]{1,0:T(8,128)S(1)} %bitcast.5, f32[1,128]{1,0:T(1,128)S(1)} %bitcast.6, f32[1,128]{1,0:T(1,128)S(1)} %bitcast.7, f32[4,8,128]{2,1,0:T(8,128)S(1)} %get-tuple-element.33.cosine, ...), custom_call_target="tpu_custom_call" | custom-call | tf_op jit(solution)/shard_map/attend/pallas_call | solution.py:198
  30.4 0.6 broadcast_in_dim.10
  31.0 3.4 %all-to-all-start.1 = ((f32[8,24,128]{2,1,0:T(8,128)}), f32[8,24,128]{2,1,0:T(8,128)S(1)}, u32[]{:S(2)}, u32[]{:S(2)}) async-start(f32[8,24,128]{2,1,0:T(8,128)} %broadcast_in_dim.10), calls=%async_computation.1 | async-start | bytes 196608 | tf_op jit(solution)/shard_map/all_to_all | solution.py:413
  34.4 1.3 %collective-permute-start.1 = (bf16[16,16,256]{2,1,0:T(8,128)(2,1)}, bf16[16,16,256]{2,1,0:T(8,128)(2,1)S(1)}, u32[]{:S(2)}, u32[]{:S(2)}) collective-permute-start(bf16[16,16,256]{2,1,0:T(8,128)(2,1)} %get-tuple-element.24.refs_1_), channel_id=1, source_target_pairs={{16,0},{20,4},{24,8},{28,12},{17,1},{21,5},{25,9},{29,13},{18,2},{... | collective-permute-start | bytes 393224 | tf_op jit(solution)/shard_map/ppermute | solution.py:386
  35.7 10.1 %collective-permute-done.1.refs_1_ = bf16[16,16,256]{2,1,0:T(8,128)(2,1)S(1)} collective-permute-done((bf16[16,16,256]{2,1,0:T(8,128)(2,1)}, bf16[16,16,256]{2,1,0:T(8,128)(2,1)S(1)}, u32[]{:S(2)}, u32[]{:S(2)}) %collective-permute-start.1) | collective-permute-done | bytes 131104 | tf_op jit(solution)/shard_map/ppermute | solution.py:386
  45.8 0.0 copy-start.9
  45.8 0.0 all-to-all-done.1.parts
  45.8 1.3 %collective-permute-start.3 = (bf16[96,16,256]{2,1,0:T(8,128)(2,1)}, bf16[96,16,256]{2,1,0:T(8,128)(2,1)S(1)}, u32[]{:S(2)}, u32[]{:S(2)}) collective-permute-start(bf16[96,16,256]{2,1,0:T(8,128)(2,1)} %get-tuple-element.26.refs_2_), channel_id=1, source_target_pairs={{16,0},{20,4},{24,8},{28,12},{17,1},{21,5},{25,9},{29,13},{18,2},{... | collective-permute-start | bytes 2359304 | tf_op jit(solution)/shard_map/ppermute | solution.py:386
  47.1 0.0 copy-done
  47.1 0.5 project.1
  47.6 1.5 %collective-permute-start.2 = (f32[2,4,1024]{2,1,0:T(4,128)S(1)}, f32[2,4,1024]{2,1,0:T(4,128)S(1)}, u32[]{:S(2)}, u32[]{:S(2)}) collective-permute-start(f32[2,4,1024]{2,1,0:T(4,128)S(1)} %project.1), channel_id=1, source_target_pairs={{0,2},{2,0},{1,3},{3,1},{4,6},{6,4},{5,7},{7,5},{8,10},{10,8},{9,1... | collective-permute-start | bytes 98312 | tf_op jit(solution)/shard_map/ppermute | solution.py:419
  49.1 0.0 copy-done.10
  49.1 0.1 copy.16.plan
  49.2 0.0 copy-done.8
  49.2 0.0 copy-done.9
  49.2 0.0 copy-done.2
  49.2 5.2 %copy_pool.1.base = bf16[512,16,256]{2,1,0:T(8,128)(2,1)} custom-call(s32[1,512]{1,0:T(1,128)S(1)} %copy-done.2, s32[4]{0:T(128)S(1)} %copy-done.4, s32[4,2]{1,0:T(4,128)S(1)} %copy.16.plan, f32[8,256]{1,0:T(8,128)S(1)} %get-tuple-element.27.entries, bf16[512,16,256]{2,1,0:T(8,128)(2,1)} %bitcast.9, bf16[16,16,256]{2,1,0:T(8,128)(2,1)} %copy-done.8, ...), custom_call_target="tpu_custom_call" | custom-call | tf_op jit(solution)/shard_map/copy_pool/pallas_call | solution.py:323
  54.4 0.0 collective-permute-done.2
  54.4 0.6 add.23
  55.0 26.2 %collective-permute-done.3.pages = bf16[96,16,256]{2,1,0:T(8,128)(2,1)S(1)} collective-permute-done((bf16[96,16,256]{2,1,0:T(8,128)(2,1)}, bf16[96,16,256]{2,1,0:T(8,128)(2,1)S(1)}, u32[]{:S(2)}, u32[]{:S(2)}) %collective-permute-start.3) | collective-permute-done | bytes 786464 | tf_op jit(solution)/shard_map/ppermute | solution.py:386
  81.2 1.6 %finish.1 = bf16[512,16,256]{2,1,0:T(8,128)(2,1)} custom-call(s32[1,512]{1,0:T(1,128)S(1)} %copy-done.2, s32[4,2]{1,0:T(4,128)S(1)} %copy.16.plan, bf16[96,16,256]{2,1,0:T(8,128)(2,1)S(1)} %collective-permute-done.3.pages, bf16[512,16,256]{2,1,0:T(8,128)(2,1)} %copy_pool.1.base), custom_call_target="tpu_custom_call", output_to_operand_aliasing={{}: (3, {})} | custom-call | tf_op jit(solution)/shard_map/finish/pallas_call | solution.py:362
  (2 shorter events, 0.0 us)
Async XLA Ops:
  0.6 16.5 %copy-start.4 = (s32[4]{0:T(128)S(1)}, s32[4]{0:T(128)}, u32[]{:S(2)}) copy-start(s32[4]{0:T(128)} %lengths.3) | copy-start | bytes 52
  0.6 26.5 %copy-start.7 = (f32[128]{0:T(128)S(1)}, f32[128]{0:T(128)}, u32[]{:S(2)}) copy-start(f32[128]{0:T(128)} %param.18) | copy-start | bytes 1540
  0.7 26.5 %copy-start.6 = (f32[128]{0:T(128)S(1)}, f32[128]{0:T(128)}, u32[]{:S(2)}) copy-start(f32[128]{0:T(128)} %param.16) | copy-start | bytes 1540
  0.7 0.7 copy-start.1
  1.4 0.7 copy-start.3
  2.1 25.1 %copy-start.5 = (f32[1024]{0:T(1024)S(1)}, f32[1024]{0:T(1024)}, u32[]{:S(2)}) copy-start(f32[1024]{0:T(1024)} %param.14) | copy-start | bytes 12292
  2.1 45.0 %copy-start = (bf16[1024,1024]{1,0:T(8,128)(2,1)S(1)}, bf16[1024,1024]{1,0:T(8,128)(2,1)}, u32[]{:S(2)}) copy-start(bf16[1024,1024]{1,0:T(8,128)(2,1)} %w_out.1) | copy-start | bytes 6291460
  8.5 40.6 %copy-start.10 = (s32[4,2]{0,1:T(2,128)S(1)}, s32[4,2]{0,1:T(2,128)}, u32[]{:S(2)}) copy-start(s32[4,2]{0,1:T(2,128)} %param.23) | copy-start | bytes 100
  8.5 40.7 %copy-start.2 = (s32[1,512]{1,0:T(1,128)S(1)}, s32[1,512]{1,0:T(1,128)}, u32[]{:S(2)}) copy-start(s32[1,512]{1,0:T(1,128)} %table.5) | copy-start | bytes 6148
  8.6 18.6 %all-to-all-start = ((f32[8,2,1280]{2,1,0:T(2,128)}), f32[8,2,1280]{2,1,0:T(2,128)S(1)}, u32[]{:S(2)}, u32[]{:S(2)}) async-start(f32[8,2,1280]{2,1,0:T(2,128)} %get-tuple-element.16), calls=%async_computation | async-start | bytes 163840 | tf_op jit(solution)/shard_map/all_to_all | solution.py:389
  15.8 11.3 %collective-permute-start = (bf16[16,16,256]{2,1,0:T(8,128)(2,1)}, bf16[16,16,256]{2,1,0:T(8,128)(2,1)S(1)}, u32[]{:S(2)}, u32[]{:S(2)}) collective-permute-start(bf16[16,16,256]{2,1,0:T(8,128)(2,1)} %get-tuple-element.17.refs_0_), channel_id=1, source_target_pairs={{16,0},{20,4},{24,8},{28,12},{17,1},{21,5},{25,9},{29,13},{18,2},{... | collective-permute-start | bytes 393224 | tf_op jit(solution)/shard_map/ppermute | solution.py:388
  27.1 22.1 %copy-start.8 = (bf16[16,16,256]{2,1,0:T(8,128)(2,1)}, bf16[16,16,256]{2,1,0:T(8,128)(2,1)S(1)}, u32[]{:S(2)}) copy-start(bf16[16,16,256]{2,1,0:T(8,128)(2,1)S(1)} %collective-permute-done.refs_0_) | copy-start | bytes 393220
  31.0 14.8 %all-to-all-start.1 = ((f32[8,24,128]{2,1,0:T(8,128)}), f32[8,24,128]{2,1,0:T(8,128)S(1)}, u32[]{:S(2)}, u32[]{:S(2)}) async-start(f32[8,24,128]{2,1,0:T(8,128)} %broadcast_in_dim.10), calls=%async_computation.1 | async-start | bytes 196608 | tf_op jit(solution)/shard_map/all_to_all | solution.py:413
  34.4 11.4 %collective-permute-start.1 = (bf16[16,16,256]{2,1,0:T(8,128)(2,1)}, bf16[16,16,256]{2,1,0:T(8,128)(2,1)S(1)}, u32[]{:S(2)}, u32[]{:S(2)}) collective-permute-start(bf16[16,16,256]{2,1,0:T(8,128)(2,1)} %get-tuple-element.24.refs_1_), channel_id=1, source_target_pairs={{16,0},{20,4},{24,8},{28,12},{17,1},{21,5},{25,9},{29,13},{18,2},{... | collective-permute-start | bytes 393224 | tf_op jit(solution)/shard_map/ppermute | solution.py:386
  45.8 3.4 %copy-start.9 = (bf16[16,16,256]{2,1,0:T(8,128)(2,1)}, bf16[16,16,256]{2,1,0:T(8,128)(2,1)S(1)}, u32[]{:S(2)}) copy-start(bf16[16,16,256]{2,1,0:T(8,128)(2,1)S(1)} %collective-permute-done.1.refs_1_) | copy-start | bytes 393220
  45.8 35.4 %collective-permute-start.3 = (bf16[96,16,256]{2,1,0:T(8,128)(2,1)}, bf16[96,16,256]{2,1,0:T(8,128)(2,1)S(1)}, u32[]{:S(2)}, u32[]{:S(2)}) collective-permute-start(bf16[96,16,256]{2,1,0:T(8,128)(2,1)} %get-tuple-element.26.refs_2_), channel_id=1, source_target_pairs={{16,0},{20,4},{24,8},{28,12},{17,1},{21,5},{25,9},{29,13},{18,2},{... | collective-permute-start | bytes 2359304 | tf_op jit(solution)/shard_map/ppermute | solution.py:386
  47.6 6.8 %collective-permute-start.2 = (f32[2,4,1024]{2,1,0:T(4,128)S(1)}, f32[2,4,1024]{2,1,0:T(4,128)S(1)}, u32[]{:S(2)}, u32[]{:S(2)}) collective-permute-start(f32[2,4,1024]{2,1,0:T(4,128)S(1)} %project.1), channel_id=1, source_target_pairs={{0,2},{2,0},{1,3},{3,1},{4,6},{6,4},{5,7},{7,5},{8,10},{10,8},{9,1... | collective-permute-start | bytes 98312 | tf_op jit(solution)/shard_map/ppermute | solution.py:419

commit v2 on v1

--- a/solution.py
+++ b/solution.py
@@ -11,8 +11,7 @@
 STEPS = 2
 SECTION = 64
 MOVED_MAX = STEPS * SECTION
-PIECES = (16, 16, 96, 128, 128)
-MOVED_PIECES = 3
+PIECES = (16, 16, 96)
 CHUNKS = 8
 NEG = -1e30
 
@@ -31,56 +30,47 @@
     return pltpu.CompilerParams(vmem_limit_bytes=mib * 1024 * 1024)
 
 
-def prepare_kernel(
-    table, normed, w_query, w_key, w_value, pool, partial, *refs
-):
-    pieces, (held, order, w_all, sems, out_sems, w_sems) = refs[: len(refs) - 6], refs[len(refs) - 6 :]
-    slots = held.shape[0]
-    per = slots // CHUNKS
+def prepare_kernel(table_in, normed_in, w_query, w_key, w_value, pool, partial, *refs):
+    pieces, (table, normed, weights, table_sem, sems, page_sems) = refs[:-6], refs[-6:]
     pairs = partial.shape[0]
     requests = pairs // 2
-    head = w_key.shape[1]
-
-    weights = []
-    start = 0
+    table_copy = pltpu.make_async_copy(table_in, table, table_sem)
+    table_copy.start()
+    loads = [pltpu.make_async_copy(normed_in, normed, sems.at[3])]
+    low = 0
     for i, weight in enumerate((w_query, w_key, w_value)):
-        part = w_all.at[:, start : start + weight.shape[1]]
-        weights.append(pltpu.make_async_copy(weight, part, w_sems.at[i]))
-        start += weight.shape[1]
-
-    def fetch(c):
-        part = pl.ds(c * per, per)
-        return pltpu.make_async_copy(pool.at[part], held.at[part], sems.at[c])
-
-    for copy in weights:
+        part = weights.at[:, low : low + weight.shape[1]]
+        loads.append(pltpu.make_async_copy(weight, part, sems.at[i]))
+        low += weight.shape[1]
+    for copy in loads:
         copy.start()
-    for c in range(CHUNKS):
-        fetch(c).start()
+    table_copy.wait()
+
+    @pl.when(lax.axis_index("pair") >= requests)
+    def _():
+        low = 0
+        for i, piece in enumerate(pieces):
+
+            def start(j, carry):
+                pltpu.make_async_copy(pool.at[table[0, low + j]], piece.at[j], page_sems.at[i]).start()
+                return carry
+
+            lax.fori_loop(0, piece.shape[0], start, 0, unroll=8)
+            low += piece.shape[0]
+
+    for copy in loads:
+        copy.wait()
     hidden = jnp.concatenate([normed[s].astype(jnp.float32) for s in range(STEPS)], 0).astype(jnp.bfloat16)
-    for copy in weights:
-        copy.wait()
-    result = jnp.dot(hidden, w_all[...], preferred_element_type=jnp.float32)
+    result = jnp.dot(hidden, weights[...], preferred_element_type=jnp.float32)
     for p in range(pairs):
         for s in range(STEPS):
             row = s * requests + p % requests
             partial[p, s : s + 1] = result[row : row + 1]
-    for c in range(CHUNKS):
-        fetch(c).wait()
-
-    def sort(j, carry):
-        order[j] = held[table[0, j]]
-        return carry
-
-    copies = []
-    low = 0
-    for i, piece in enumerate(pieces):
-        high = low + piece.shape[0]
-        lax.fori_loop(low, high, sort, 0, unroll=8)
-        copies.append(pltpu.make_async_copy(order.at[pl.ds(low, piece.shape[0])], piece, out_sems.at[i]))
-        copies[-1].start()
-        low = high
-    for copy in copies:
-        copy.wait()
+
+    @pl.when(lax.axis_index("pair") >= requests)
+    def _():
+        for i, piece in enumerate(pieces):
+            pltpu.make_async_copy(pool.at[pl.ds(0, piece.shape[0])], piece, page_sems.at[i]).wait()
 
 
 def prepare(table, normed, w_query, w_key, w_value, pool, pairs):
@@ -89,33 +79,43 @@
     return pl.pallas_call(
         prepare_kernel,
         out_shape=(jax.ShapeDtypeStruct((pairs, STEPS, wide), jnp.float32),)
-        + tuple(pltpu.HBM((n,) + page, pool.dtype) for n in PIECES),
-        in_specs=[SMEM, VMEM, HBM, HBM, HBM, HBM],
-        out_specs=(VMEM,) + (HBM,) * len(PIECES),
+        + tuple(pltpu.VMEM((n,) + page, pool.dtype) for n in PIECES),
+        in_specs=[HBM] * 6,
+        out_specs=(VMEM,) + (VMEM,) * len(PIECES),
         scratch_shapes=[
-            pltpu.VMEM(pool.shape, pool.dtype),
-            pltpu.VMEM((PAGES_HALF,) + page, pool.dtype),
+            pltpu.SMEM(table.shape, table.dtype),
+            pltpu.VMEM(normed.shape, normed.dtype),
             pltpu.VMEM((w_query.shape[0], wide), w_query.dtype),
-            pltpu.SemaphoreType.DMA((CHUNKS,)),
+            pltpu.SemaphoreType.DMA,
+            pltpu.SemaphoreType.DMA((4,)),
             pltpu.SemaphoreType.DMA((len(PIECES),)),
-            pltpu.SemaphoreType.DMA((3,)),
         ],
-        compiler_params=params(24),
+        compiler_params=params(16),
         name="prepare",
-    )(table, normed, *in_hbm(w_query, w_key, w_value, pool))
-
-
-def attention_kernel(lengths, sums, b_query, b_key, b_value, cosine, sine, *refs):
-    pieces, (packed, entries, held, score, sems) = refs[: len(PIECES)], refs[len(PIECES) :]
+    )(*in_hbm(table, normed, w_query, w_key, w_value, pool))
+
+
+def page_order(table, slots):
+    slot = lax.broadcasted_iota(jnp.int32, (slots, slots), 0)
+    holds = jnp.where(slot == table, 1.0, 0.0).astype(jnp.bfloat16)
+    index = lax.broadcasted_iota(jnp.int32, (8, slots), 1)
+    digit = lax.broadcasted_iota(jnp.int32, (8, slots), 0)
+    digits = jnp.where(digit == 0, index // 16, jnp.where(digit == 1, index % 16, 0))
+    digits = digits.astype(jnp.float32).astype(jnp.bfloat16)
+    return lax.dot_general(digits, holds, (((1,), (1,)), ((), ())), preferred_element_type=jnp.float32)
+
+
+def attention_kernel(
+    lengths, table, sums, b_query, b_key, b_value, cosine, sine, pool, packed, entries, held, score, sems
+):
+    slots, page_len, _ = held.shape
+    per = slots // CHUNKS
     copies = []
-    low = 0
-    for i, piece in enumerate(pieces):
-        size = piece.shape[0]
-        copies.append((low, pltpu.make_async_copy(piece, held.at[pl.ds(low, size)], sems.at[i])))
-        copies[-1][1].start()
-        low += size
+    for c in range(CHUNKS):
+        part = pl.ds(c * per, per)
+        copies.append(pltpu.make_async_copy(pool.at[part], held.at[part], sems.at[c]))
+        copies[-1].start()
     requests = sums.shape[0] // 2
-    page_len = held.shape[1]
     group, head = b_query.shape
     rows = STEPS * group
     pair_index = lax.axis_index("pair")
@@ -123,6 +123,19 @@
     request = jnp.where(is_source, pair_index - requests, pair_index)
     half_tokens = PAGES_HALF * page_len
     limit = jnp.where(is_source, lengths[request] - half_tokens, half_tokens)
+
+    blocks = CHUNKS // 2
+    block = slots // blocks
+    width = block * page_len
+    digits = page_order(table[...], slots)
+    digits = jnp.concatenate(
+        [digits[d : d + 1, c * block : (c + 1) * block] for d in range(2) for c in range(blocks)], 0
+    ).astype(jnp.bfloat16)
+    spread = lax.broadcasted_iota(jnp.int32, (block, width), 1) // page_len
+    spread = jnp.where(spread == lax.broadcasted_iota(jnp.int32, (block, width), 0), 1.0, 0.0)
+    digits = jnp.dot(digits, spread.astype(jnp.bfloat16), preferred_element_type=jnp.float32)
+    tokens = (digits[:blocks] * 16.0 + digits[blocks:]).astype(jnp.int32) * page_len
+    tokens = tokens + lax.broadcasted_iota(jnp.int32, (blocks, width), 1) % page_len
 
     total = sums[0]
     for p in range(1, sums.shape[0]):
@@ -157,17 +170,12 @@
         fresh.append((jnp.where(seen, dots, NEG), seen))
     row_max = jnp.maximum(fresh[0][0], fresh[1][0])
 
-    per = 64
-    width = per * page_len
-    blocks = PAGES_HALF // per
-    lane = lax.broadcasted_iota(jnp.int32, (rows, width), 1)
     for c in range(blocks):
-        low, high = c * per, (c + 1) * per
-        while copies and copies[0][0] < high:
-            copies.pop(0)[1].wait()
-        keys = held[low:high, :, :head].reshape(width, head)
+        copies[2 * c].wait()
+        copies[2 * c + 1].wait()
+        keys = held[c * block : (c + 1) * block, :, :head].reshape(width, head)
         part = lax.dot_general(query, keys, (((1,), (1,)), ((), ())), preferred_element_type=jnp.float32)
-        part = jnp.where(lane < limit - c * width, part * scale, NEG)
+        part = jnp.where(tokens[c : c + 1] < limit, part * scale, NEG)
         score[:, c * width : (c + 1) * width] = part
         row_max = jnp.maximum(row_max, jnp.max(part, 1, keepdims=True))
     row_sum = jnp.zeros((rows, 1), jnp.float32)
@@ -177,40 +185,39 @@
         row_sum = row_sum + weight
         out = out + weight.astype(jnp.bfloat16).astype(jnp.float32) * value_new[s : s + 1]
     for c in range(blocks):
-        low, high = c * per, (c + 1) * per
         weight = jnp.exp(score[:, c * width : (c + 1) * width] - row_max)
-        weight = jnp.where(lane < limit - c * width, weight, 0.0)
+        weight = jnp.where(tokens[c : c + 1] < limit, weight, 0.0)
         row_sum = row_sum + jnp.sum(weight, 1, keepdims=True)
-        values = held[low:high, :, head:].reshape(width, head)
+        values = held[c * block : (c + 1) * block, :, head:].reshape(width, head)
         out = out + jnp.dot(weight.astype(jnp.bfloat16), values, preferred_element_type=jnp.float32)
 
     diagonal = lax.broadcasted_iota(jnp.int32, (rows, head), 1) == row
-    packed[0:rows] = out
-    packed[rows : rows + 1] = jnp.sum(jnp.where(diagonal, row_max, 0.0), 0, keepdims=True)
-    packed[rows + 1 : rows + 2] = jnp.sum(jnp.where(diagonal, row_sum, 0.0), 0, keepdims=True)
-    packed[rows + 2 :] = jnp.zeros((packed.shape[0] - rows - 2, head), jnp.float32)
-
-
-def attend(lengths, sums, b_query, b_key, b_value, cosine, sine, pieces):
+    for p in range(packed.shape[0]):
+        packed[p, 0:rows] = out
+        packed[p, rows : rows + 1] = jnp.sum(jnp.where(diagonal, row_max, 0.0), 0, keepdims=True)
+        packed[p, rows + 1 : rows + 2] = jnp.sum(jnp.where(diagonal, row_sum, 0.0), 0, keepdims=True)
+        packed[p, rows + 2 :] = jnp.zeros((packed.shape[1] - rows - 2, head), jnp.float32)
+
+
+def attend(lengths, table, sums, b_query, b_key, b_value, cosine, sine, pool):
     group, head = b_query.shape
     rows = STEPS * group
-    page = pieces[0].shape[1:]
     return pl.pallas_call(
         attention_kernel,
         out_shape=(
-            jax.ShapeDtypeStruct((rows + 8, head), jnp.float32),
+            jax.ShapeDtypeStruct((sums.shape[0], rows + 8, head), jnp.float32),
             jax.ShapeDtypeStruct((8, 2 * head), jnp.float32),
         ),
-        in_specs=[SMEM] + [VMEM] * 6 + [HBM] * len(pieces),
+        in_specs=[SMEM] + [VMEM] * 7 + [HBM],
         out_specs=(VMEM, VMEM),
         scratch_shapes=[
-            pltpu.VMEM((PAGES_HALF,) + page, pieces[0].dtype),
-            pltpu.VMEM((rows, PAGES_HALF * page[0]), jnp.float32),
-            pltpu.SemaphoreType.DMA((len(pieces),)),
+            pltpu.VMEM(pool.shape, pool.dtype),
+            pltpu.VMEM((rows, pool.shape[0] * pool.shape[1]), jnp.float32),
+            pltpu.SemaphoreType.DMA((CHUNKS,)),
         ],
         compiler_params=params(24),
         name="attend",
-    )(lengths, sums, b_query, b_key, b_value, cosine, sine, *in_hbm(*pieces))
+    )(lengths, table, sums, b_query, b_key, b_value, cosine, sine, *in_hbm(pool))
 
 
 def project_kernel(parts, w_out, out):
@@ -266,7 +273,7 @@
 
 
 def copy_kernel(table, lengths, plan, entries, pool, *refs):
-    early, (new_pool, held, pages, sems, out_sems, page_sems) = refs[:-6], refs[-6:]
+    early, (new_pool, held, sems, out_sems) = refs[:-4], refs[-4:]
     slots, page_len, width = held.shape
     per = slots // CHUNKS
     requests = lengths.shape[0]
@@ -283,15 +290,6 @@
 
     for c in range(CHUNKS):
         fetch(c).start()
-    copies = []
-    low = 0
-    for i, piece in enumerate(early):
-        size = piece.shape[0]
-        copies.append(pltpu.make_async_copy(piece, pages.at[pl.ds(low, size)], page_sems.at[i]))
-        copies[-1].start()
-        low += size
-    for copy in copies:
-        copy.wait()
     for c in range(CHUNKS):
         fetch(c).wait()
 
@@ -307,11 +305,16 @@
 
     @pl.when(jnp.logical_not(is_source))
     def _():
-        def place(j, carry):
-            held[table[0, PAGES_HALF + j]] = pages[j]
-            return carry
-
-        lax.fori_loop(0, jnp.minimum(moved_pages(plan, pair_index), pages.shape[0]), place, 0)
+        count = moved_pages(plan, pair_index)
+        low = 0
+        for pages in early:
+
+            def place(j, carry):
+                held[table[0, PAGES_HALF + low + j]] = pages[j]
+                return carry
+
+            lax.fori_loop(0, jnp.clip(count - low, 0, pages.shape[0]), place, 0)
+            low += pages.shape[0]
 
     for c in range(CHUNKS):
         store(c).start()
@@ -323,18 +326,16 @@
     return pl.pallas_call(
         copy_kernel,
         out_shape=jax.ShapeDtypeStruct(pool.shape, pool.dtype),
-        in_specs=[SMEM, SMEM, SMEM, VMEM, HBM] + [HBM] * len(early),
+        in_specs=[SMEM, SMEM, SMEM, VMEM, HBM] + [VMEM] * len(early),
         out_specs=HBM,
         scratch_shapes=[
             pltpu.VMEM(pool.shape, pool.dtype),
-            pltpu.VMEM((sum(PIECES[: MOVED_PIECES - 1]),) + pool.shape[1:], pool.dtype),
             pltpu.SemaphoreType.DMA((CHUNKS,)),
             pltpu.SemaphoreType.DMA((CHUNKS,)),
-            pltpu.SemaphoreType.DMA((len(early),)),
         ],
         compiler_params=params(24),
         name="copy_pool",
-    )(table, lengths, plan, entries, *in_hbm(pool, *early))
+    )(table, lengths, plan, entries, *in_hbm(pool), *early)
 
 
 def finish_kernel(table, plan, pages, base, new_pool, sem):
@@ -387,7 +388,6 @@
 
     incoming = [lax.ppermute(pieces[0], "pair", route)]
     sums = lax.all_to_all(partial, "pair", split_axis=0, concat_axis=0, tiled=True)
-    sums, incoming[0] = lax.optimization_barrier((sums, incoming[0]))
     incoming.append(migrate(pieces[1], sums))
 
     frequency = rope_base ** (-(jnp.arange(head // 2, dtype=jnp.float32) * 2.0 / head))
@@ -401,17 +401,16 @@
 
     packed, entries = attend(
         lengths,
+        page_table,
         sums,
         b_query.reshape(-1, head),
         b_key[None, :],
         b_value[None, :],
         cosine,
         sine,
-        pieces,
+        pool[0, 0],
     )
-    spread = jnp.broadcast_to(packed[None], (pair_count,) + packed.shape)
-    parts = lax.all_to_all(spread, "pair", split_axis=0, concat_axis=0, tiled=True)
-    parts, incoming[1] = lax.optimization_barrier((parts, incoming[1]))
+    parts = lax.all_to_all(packed, "pair", split_axis=0, concat_axis=0, tiled=True)
     incoming.append(migrate(pieces[2], parts))
     new_pool = copy_pool(page_table, lengths, plan, entries, pool[0, 0], incoming[:-1])
     projected = project(parts, w_out)

time: 83.3 us -> 86.8 us (1.042)
  blocking collectives: 0 us -> 9.51 us
  Pallas kernels: 16.9 us -> 13.9 us
  starting transfers between devices: 16 us -> 13.2 us
  local copies, waits for them, and re-layouts: 2.19 us -> 0.12 us
  waiting for transfers between devices: 46 us -> 48 us
    ppermute x2, waiting for transfers between devices: 36.3 us -> 2.72 us  [migrate(): lax.ppermute(lax.optimization_barrier((pages, after))[0], 'pair', route)]
    ppermute x1, waiting for transfers between devices: 9.68 us -> 38.5 us  [local(): incoming = [lax.ppermute(pieces[0], 'pair', route)]]
    all_to_all x0 -> x1, blocking collectives: none -> 9.51 us  [local(): lax.all_to_all(packed, 'pair', split_axis=0, concat_axis=0, tiled=True)]
    all_to_all x1, waiting for transfers between devices: 0.01 us -> 6.68 us  [local(): lax.all_to_all(partial, 'pair', split_axis=0, concat_axis=0, tiled=True)]
    all_to_all x1 -> x0, starting transfers between devices: 3.36 us -> none  [local(): lax.all_to_all(spread, 'pair', split_axis=0, concat_axis=0, tiled=True)]
    pallas_call x1, Pallas kernels: 6.44 us -> 3.29 us  [prepare(): pl.pallas_call(prepare_kernel, out_shape=(jax.ShapeDtypeStruct((pairs, ST...]
    unnamed x23 -> x15, local copies, waits for them, and re-layouts: 1.54 us -> 0.12 us
  transfers between devices with their start and end apart: 6 -> 5, of which waited for: 3 -> 3; matrix products, arithmetic and copies ran while one was open for 1% -> 1% of each run, Pallas kernels for 7% -> 6%
where the time goes in v2:
time: 86.8 us; the launch traced here: 86.5 us
  waiting for transfers between devices  48 us (55%)
  Pallas kernels  13.9 us (16%)
  starting transfers between devices  13.2 us (15%)
  blocking collectives  9.51 us (11%)
  other arithmetic  0.93 us (1%)
    ppermute x1, waiting for transfers between devices, local(): incoming = [lax.ppermute(pieces[0], 'pair', route)]  38.5 us
    all_to_all x1, blocking collectives, local(): lax.all_to_all(packed, 'pair', split_axis=0, concat_axis=0, tiled=True)  9.51 us
    all_to_all x1, starting transfers between devices, local(): lax.all_to_all(partial, 'pair', split_axis=0, concat_axis=0, tiled=True)  7.85 us
    all_to_all x1, waiting for transfers between devices, local(): lax.all_to_all(partial, 'pair', split_axis=0, concat_axis=0, tiled=True)  6.68 us
    pallas_call x1, Pallas kernels, copy_pool(): pl.pallas_call(copy_kernel, out_shape=jax.ShapeDtypeStruct(pool.shape, po...  5.04 us
    pallas_call x1, Pallas kernels, attend(): pl.pallas_call(attention_kernel, out_shape=(jax.ShapeDtypeStruct((sums.sh...  3.72 us
    pallas_call x1, Pallas kernels, prepare(): pl.pallas_call(prepare_kernel, out_shape=(jax.ShapeDtypeStruct((pairs, ST...  3.29 us
    ppermute x2, waiting for transfers between devices, migrate(): lax.ppermute(lax.optimization_barrier((pages, after))[0], 'pair', route)  2.72 us
  transfers between devices with their start and end apart: 5, of which 3 were waited for; matrix products, arithmetic and copies ran while one was open for 1% of the time, Pallas kernels for 6%

profile of v2, /device:TPU:0, one launch (start us, length us, event | category | flops | bytes accessed | tf_op | source)
XLA Modules:
  0.0 86.5 jit_solution(13215891196156085645)
XLA Ops:
  0.6 0.0 copy-start.1
  0.6 0.0 copy-start.2
  0.7 0.0 copy-start.5
  0.7 0.0 copy-start.4
  0.7 0.0 copy-start.3
  0.7 0.0 copy-start
  0.7 3.3 %prepare.1 = (f32[8,2,1280]{2,1,0:T(2,128)}, bf16[16,16,256]{2,1,0:T(8,128)(2,1)S(1)}, bf16[16,16,256]{2,1,0:T(8,128)(2,1)S(1)}, bf16[96,16,256]{2,1,0:T(8,128)(2,1)}) custom-call(s32[1,512]{1,0:T(1,128)} %table.5, bf16[2,4,1024]{2,1,0:T(4,128)(2,1)} %normed_in.1, bf16[1024,1024]{1,0:T(8,128)(2,1)} %w_query.1, bf16[1024,128]{1,0:T(8,128)(2,1)} %w_key.1, ...), custom_call_target="tpu_custom_call" | custom-call | tf_op jit(solution)/shard_map/prepare/pallas_call | solution.py:79
  4.0 0.0 copy-start.6
  4.0 7.9 %all-to-all-start = ((f32[8,2,1280]{2,1,0:T(2,128)}), f32[8,2,1280]{2,1,0:T(2,128)S(1)}, u32[]{:S(2)}, u32[]{:S(2)}) async-start(f32[8,2,1280]{2,1,0:T(2,128)} %get-tuple-element.10), calls=%async_computation | async-start | bytes 163840 | tf_op jit(solution)/shard_map/all_to_all | solution.py:390
  11.9 0.0 copy-done.2
  11.9 0.1 add_convert_fusion
  12.0 0.1 fusion
  12.1 0.1 pad_maximum_fusion
  12.2 6.7 %all-to-all-done.sums = f32[8,2,1280]{2,1,0:T(2,128)S(1)} async-done(((f32[8,2,1280]{2,1,0:T(2,128)}), f32[8,2,1280]{2,1,0:T(2,128)S(1)}, u32[]{:S(2)}, u32[]{:S(2)}) %all-to-all-start) | async-done | bytes 81952 | tf_op jit(solution)/shard_map/all_to_all | solution.py:390
  18.9 0.0 copy-done.1
  18.9 0.0 copy-done.5
  18.9 0.0 copy-done.4
  18.9 0.0 copy-done.3
  18.9 3.7 %attend.1 = (f32[8,24,128]{2,1,0:T(8,128)S(1)}, f32[8,256]{1,0:T(8,128)S(1)}) custom-call(s32[4]{0:T(128)S(1)} %copy-done.2, s32[1,512]{1,0:T(1,128)S(1)} %copy-done.1, f32[8,2,1280]{2,1,0:T(2,128)S(1)} %all-to-all-done.sums, f32[8,128]{1,0:T(8,128)S(1)} %bitcast.5, f32[1,128]{1,0:T(1,128)S(1)} %bitcast.6, f32[1,128]{1,0:T(1,128)S(1)} %bitcast.7, ...), custom_call_target="tpu_custom_call" | custom-call | tf_op jit(solution)/shard_map/attend/pallas_call | solution.py:205
  22.6 9.5 %all_to_all.10.parts = f32[8,24,128]{2,1,0:T(8,128)S(1)} all-to-all(f32[8,24,128]{2,1,0:T(8,128)S(1)} %get-tuple-element.11), channel_id=1, replica_groups=mesh['pair'=8,'tp'=2,'rep'=2] {'pair'}, dimensions={0} | all-to-all | bytes 196608 | tf_op jit(solution)/shard_map/all_to_all | solution.py:413
  32.1 1.3 %collective-permute-start.1 = (bf16[96,16,256]{2,1,0:T(8,128)(2,1)}, bf16[96,16,256]{2,1,0:T(8,128)(2,1)S(1)}, u32[]{:S(2)}, u32[]{:S(2)}) collective-permute-start(bf16[96,16,256]{2,1,0:T(8,128)(2,1)} %get-tuple-element.13), channel_id=1, source_target_pairs={{16,0},{20,4},{24,8},{28,12},{17,1},{21,5},{25,9},{29,13},{18,2},{... | collective-permute-start | bytes 2359304 | tf_op jit(solution)/shard_map/ppermute | solution.py:387
  33.4 1.3 %collective-permute-start.2 = (bf16[16,16,256]{2,1,0:T(8,128)(2,1)S(1)}, bf16[16,16,256]{2,1,0:T(8,128)(2,1)S(1)}, u32[]{:S(2)}, u32[]{:S(2)}) collective-permute-start(bf16[16,16,256]{2,1,0:T(8,128)(2,1)S(1)} %get-tuple-element.15), channel_id=1, source_target_pairs={{16,0},{20,4},{24,8},{28,12},{17,1},{21,5},{25,9},{29,13},{18,2},{... | collective-permute-start | bytes 393224 | tf_op jit(solution)/shard_map/ppermute | solution.py:389
  34.7 1.3 %collective-permute-start.3 = (bf16[16,16,256]{2,1,0:T(8,128)(2,1)S(1)}, bf16[16,16,256]{2,1,0:T(8,128)(2,1)S(1)}, u32[]{:S(2)}, u32[]{:S(2)}) collective-permute-start(bf16[16,16,256]{2,1,0:T(8,128)(2,1)S(1)} %get-tuple-element.17), channel_id=1, source_target_pairs={{16,0},{20,4},{24,8},{28,12},{17,1},{21,5},{25,9},{29,13},{18,2},{... | collective-permute-start | bytes 393224 | tf_op jit(solution)/shard_map/ppermute | solution.py:387
  36.0 0.0 copy-done
  36.0 0.5 project.1
  36.5 1.5 %collective-permute-start = (f32[2,4,1024]{2,1,0:T(4,128)S(1)}, f32[2,4,1024]{2,1,0:T(4,128)S(1)}, u32[]{:S(2)}, u32[]{:S(2)}) collective-permute-start(f32[2,4,1024]{2,1,0:T(4,128)S(1)} %project.1), channel_id=1, source_target_pairs={{0,2},{2,0},{1,3},{3,1},{4,6},{6,4},{5,7},{7,5},{8,10},{10,8},{9,1... | collective-permute-start | bytes 98312 | tf_op jit(solution)/shard_map/ppermute | solution.py:418
  38.0 0.0 copy-done.6
  38.0 0.1 copy.16.plan
  38.1 38.5 %collective-permute-done.2.refs_0_ = bf16[16,16,256]{2,1,0:T(8,128)(2,1)S(1)} collective-permute-done((bf16[16,16,256]{2,1,0:T(8,128)(2,1)S(1)}, bf16[16,16,256]{2,1,0:T(8,128)(2,1)S(1)}, u32[]{:S(2)}, u32[]{:S(2)}) %collective-permute-start.2) | collective-permute-done | bytes 131104 | tf_op jit(solution)/shard_map/ppermute | solution.py:389
  76.7 2.7 %collective-permute-done.3.refs_1_ = bf16[16,16,256]{2,1,0:T(8,128)(2,1)S(1)} collective-permute-done((bf16[16,16,256]{2,1,0:T(8,128)(2,1)S(1)}, bf16[16,16,256]{2,1,0:T(8,128)(2,1)S(1)}, u32[]{:S(2)}, u32[]{:S(2)}) %collective-permute-start.3) | collective-permute-done | bytes 131104 | tf_op jit(solution)/shard_map/ppermute | solution.py:387
  79.4 5.0 %copy_pool.1.base = bf16[512,16,256]{2,1,0:T(8,128)(2,1)} custom-call(s32[1,512]{1,0:T(1,128)S(1)} %copy-done.1, s32[4]{0:T(128)S(1)} %copy-done.2, s32[4,2]{1,0:T(4,128)S(1)} %copy.16.plan, f32[8,256]{1,0:T(8,128)S(1)} %get-tuple-element.14.entries, bf16[512,16,256]{2,1,0:T(8,128)(2,1)} %bitcast.10, ...), custom_call_target="tpu_custom_call" | custom-call | tf_op jit(solution)/shard_map/copy_pool/pallas_call | solution.py:326
  84.4 0.0 collective-permute-done
  84.5 0.6 add.23
  85.1 0.0 collective-permute-done.1.pages
  85.1 1.4 %finish.1 = bf16[512,16,256]{2,1,0:T(8,128)(2,1)} custom-call(s32[1,512]{1,0:T(1,128)S(1)} %copy-done.1, s32[4,2]{1,0:T(4,128)S(1)} %copy.16.plan, bf16[96,16,256]{2,1,0:T(8,128)(2,1)S(1)} %collective-permute-done.1.pages, bf16[512,16,256]{2,1,0:T(8,128)(2,1)} %copy_pool.1.base), custom_call_target="tpu_custom_call", output_to_operand_aliasing={{}: (3, {})} | custom-call | tf_op jit(solution)/shard_map/finish/pallas_call | solution.py:363
  (2 shorter events, 0.0 us)
Async XLA Ops:
  0.6 18.2 %copy-start.1 = (s32[1,512]{1,0:T(1,128)S(1)}, s32[1,512]{1,0:T(1,128)}, u32[]{:S(2)}) copy-start(s32[1,512]{1,0:T(1,128)} %table.5) | copy-start | bytes 6148
  0.6 11.2 %copy-start.2 = (s32[4]{0:T(128)S(1)}, s32[4]{0:T(128)}, u32[]{:S(2)}) copy-start(s32[4]{0:T(128)} %lengths.3) | copy-start | bytes 52
  0.7 18.2 %copy-start.5 = (f32[128]{0:T(128)S(1)}, f32[128]{0:T(128)}, u32[]{:S(2)}) copy-start(f32[128]{0:T(128)} %param.18) | copy-start | bytes 1540
  0.7 18.2 %copy-start.4 = (f32[128]{0:T(128)S(1)}, f32[128]{0:T(128)}, u32[]{:S(2)}) copy-start(f32[128]{0:T(128)} %param.16) | copy-start | bytes 1540
  0.7 18.2 %copy-start.3 = (f32[1024]{0:T(1024)S(1)}, f32[1024]{0:T(1024)}, u32[]{:S(2)}) copy-start(f32[1024]{0:T(1024)} %param.14) | copy-start | bytes 12292
  0.7 35.3 %copy-start = (bf16[1024,1024]{1,0:T(8,128)(2,1)S(1)}, bf16[1024,1024]{1,0:T(8,128)(2,1)}, u32[]{:S(2)}) copy-start(bf16[1024,1024]{1,0:T(8,128)(2,1)} %w_out.1) | copy-start | bytes 6291460
  4.0 34.0 %copy-start.6 = (s32[4,2]{0,1:T(2,128)S(1)}, s32[4,2]{0,1:T(2,128)}, u32[]{:S(2)}) copy-start(s32[4,2]{0,1:T(2,128)} %param.23) | copy-start | bytes 100
  4.0 14.9 %all-to-all-start = ((f32[8,2,1280]{2,1,0:T(2,128)}), f32[8,2,1280]{2,1,0:T(2,128)S(1)}, u32[]{:S(2)}, u32[]{:S(2)}) async-start(f32[8,2,1280]{2,1,0:T(2,128)} %get-tuple-element.10), calls=%async_computation | async-start | bytes 163840 | tf_op jit(solution)/shard_map/all_to_all | solution.py:390
  32.1 52.9 %collective-permute-start.1 = (bf16[96,16,256]{2,1,0:T(8,128)(2,1)}, bf16[96,16,256]{2,1,0:T(8,128)(2,1)S(1)}, u32[]{:S(2)}, u32[]{:S(2)}) collective-permute-start(bf16[96,16,256]{2,1,0:T(8,128)(2,1)} %get-tuple-element.13), channel_id=1, source_target_pairs={{16,0},{20,4},{24,8},{28,12},{17,1},{21,5},{25,9},{29,13},{18,2},{... | collective-permute-start | bytes 2359304 | tf_op jit(solution)/shard_map/ppermute | solution.py:387
  33.4 43.3 %collective-permute-start.2 = (bf16[16,16,256]{2,1,0:T(8,128)(2,1)S(1)}, bf16[16,16,256]{2,1,0:T(8,128)(2,1)S(1)}, u32[]{:S(2)}, u32[]{:S(2)}) collective-permute-start(bf16[16,16,256]{2,1,0:T(8,128)(2,1)S(1)} %get-tuple-element.15), channel_id=1, source_target_pairs={{16,0},{20,4},{24,8},{28,12},{17,1},{21,5},{25,9},{29,13},{18,2},{... | collective-permute-start | bytes 393224 | tf_op jit(solution)/shard_map/ppermute | solution.py:389
  34.7 44.7 %collective-permute-start.3 = (bf16[16,16,256]{2,1,0:T(8,128)(2,1)S(1)}, bf16[16,16,256]{2,1,0:T(8,128)(2,1)S(1)}, u32[]{:S(2)}, u32[]{:S(2)}) collective-permute-start(bf16[16,16,256]{2,1,0:T(8,128)(2,1)S(1)} %get-tuple-element.17), channel_id=1, source_target_pairs={{16,0},{20,4},{24,8},{28,12},{17,1},{21,5},{25,9},{29,13},{18,2},{... | collective-permute-start | bytes 393224 | tf_op jit(solution)/shard_map/ppermute | solution.py:387
  36.5 47.9 %collective-permute-start = (f32[2,4,1024]{2,1,0:T(4,128)S(1)}, f32[2,4,1024]{2,1,0:T(4,128)S(1)}, u32[]{:S(2)}, u32[]{:S(2)}) collective-permute-start(f32[2,4,1024]{2,1,0:T(4,128)S(1)} %project.1), channel_id=1, source_target_pairs={{0,2},{2,0},{1,3},{3,1},{4,6},{6,4},{5,7},{7,5},{8,10},{10,8},{9,1... | collective-permute-start | bytes 98312 | tf_op jit(solution)/shard_map/ppermute | solution.py:418
